TPU v7x, 32 devices: a whole 2x2x4 slice. The times are simulated.
32 devices in a mesh: groups: 2 (over y), replica: 4 (over x, core), tensor: 4 (over z).
Axes of the slice: x: 2, y: 2, z: 4, core: 2. Of those that a mesh axis runs over, the one named last changes fastest.
Arguments:
- tokens: bfloat16 [4096, 8192], P(('groups', 'replica'), 'tensor'), parts along dimension 0, may hold values from -6 to 6
- query_weight: bfloat16 [8192, 4096], P(None, 'tensor'), may hold values from -0.0625 to 0.0625
- adapter_down: bfloat16 [64, 8192, 64], P('replica', 'tensor'), may hold values from -0.0625 to 0.0625
- adapter_up: bfloat16 [64, 64, 4096], P('replica', None, 'tensor'), may hold values from -0.75 to 0.75
- send_table: int32 [8, 4, 2], P('groups'), parts along dimension 0, may hold values from 0 to 15, as said below
- block_slot: int32 [128], P(('groups', 'replica')), parts along dimension 0, may hold values from 0 to 7, as said below
- live_block_rows: int32 [128], P(('groups', 'replica')), parts along dimension 0, may hold values from 1 to 32, as said below
Outputs:
- queries: bfloat16 [4096, 4096], P(('groups', 'replica'), 'tensor'), parts along dimension 0
There are 2 independent parts, one for each index of `groups`. A program takes and returns all parts, laid end to end along the dimension named above; an argument that names none is the same for every part. Nothing has to cross between parts.
Inputs may be any that keep to these rules, and one draw needn't show every extreme that they name: send_table[o, r, c] names adapter o * 16 + value. `block_slot`: block k uses the piece that owner replica value // 2 sends to replica k // 16 in slot value % 2. `live_block_rows`: rows past this count in a block are padding.
All inputs are finite; a program needn't handle non-finite values.
Results may differ from a plain program's by a relative error of at most 0.0034.
Values may be sent and summed in bfloat16 or wider, within the bound.
A program may use at most 128 MiB of HBM per device.

v0:
```python
import jax
import jax.numpy as jnp
from jax import lax
from jax.sharding import PartitionSpec as P


def shards(tokens, query_weight, adapter_down, adapter_up, send_table, block_slot, live_block_rows):
    count = live_block_rows.shape[0]
    block_rows = tokens.shape[0] // count
    slots_each = send_table.shape[2]
    base = jnp.dot(
        lax.all_gather(tokens, "tensor", axis=1, tiled=True),
        query_weight,
        preferred_element_type=jnp.float32,
    )
    serving = lax.axis_index("replica")
    owner = block_slot // slots_each
    slot = block_slot % slots_each
    down_weight_all, up_all = (
        lax.all_gather(adapter_down, "replica", axis=0, tiled=True),
        lax.all_gather(adapter_up, "replica", axis=0, tiled=True),
    )
    adapter = owner * adapter_down.shape[0] + send_table[owner, serving, slot]
    down_weight_selected = down_weight_all[adapter]
    up_sel = up_all[adapter]
    block_list = tokens.reshape(count, block_rows, tokens.shape[1])
    partial_shrink = jnp.einsum(
        "zlc,zcx->zlx", block_list, down_weight_selected, preferred_element_type=jnp.float32
    )
    shrink_round = lax.psum(partial_shrink, "tensor").astype(jnp.bfloat16)
    delta = jnp.einsum("bkr,brc->bkc", shrink_round, up_sel, preferred_element_type=jnp.float32)
    live = (jnp.arange(block_rows, dtype=jnp.int32)[None, :] < live_block_rows[:, None]).astype(
        jnp.float32
    )
    delta = delta * live[:, :, None]
    return (base + delta.reshape(tokens.shape[0], query_weight.shape[1])).astype(jnp.bfloat16)


def solution(mesh):
    placed = (
        P(("groups", "replica"), "tensor"),
        P(None, "tensor"),
        P("replica", "tensor", None),
        P("replica", None, "tensor"),
        P("groups", None, None),
        P(("groups", "replica")),
        P(("groups", "replica")),
    )
    return jax.shard_map(
        shards,
        mesh=mesh,
        in_specs=placed,
        out_specs=P(("groups", "replica"), "tensor"),
        check_vma=False,
    )
```

profile of v0, /device:TPU:0, one launch (start us, length us, event | category | flops | bytes accessed | tf_op | source)
XLA Modules:
  0.0 359.3 jit_solution(10745014482374016637)
XLA Ops:
  6.5 0.0 copy-start
  6.5 0.0 copy-start.4
  6.5 0.0 all-gather.8.cloned.1.call-start
  6.5 0.7 all-gather.8.cloned.1.call-update
  7.3 0.0 all-gather.6.cloned.1.call-start
  7.3 0.7 all-gather.6.cloned.1.call-update
  8.0 0.0 all-gather.4.cloned.1.call-start
  8.1 0.7 all-gather.4.cloned.1.call-update
  8.8 0.0 copy-done.4
  8.8 0.0 copy-done
  8.8 0.7 gather_fusion
  9.5 0.0 copy-done.3
  9.5 0.1 fusion.2
  9.6 60.3 %all-gather.8.cloned.1.call-done = bf16[64,64,1024]{2,1,0:T(8,128)(2,1)} async-done(((bf16[16,64,1024]{2,1,0:T(8,128)(2,1)}), bf16[64,64,1024]{2,1,0:T(8,128)(2,1)}) %all-gather.8.cloned.1.call-update) | async-done | bytes 8388624 | tf_op jit(solution)/shard_map/all_gather | solution.py:21
  69.9 5.4 %gather_fusion.2 = bf16[16,64,1024]{2,1,0:T(8,128)(2,1)} fusion(bf16[64,64,1024]{2,1,0:T(8,128)(2,1)} %all-gather.8.cloned.1.call-done, s32[1024]{0:T(1024)S(1)} %pad_clamp_fusion), kind=kCustom, calls=%fused_computation.2 | custom fusion | bytes 4194368 | tf_op jit(solution)/shard_map/gather | solution.py:25
  75.3 102.1 %all-gather.6.cloned.1.call-done = bf16[64,2048,64]{1,2,0:T(8,128)(2,1)} async-done(((bf16[16,2048,64]{1,2,0:T(8,128)(2,1)}), bf16[64,2048,64]{1,2,0:T(8,128)(2,1)}) %all-gather.6.cloned.1.call-update) | async-done | bytes 16777232 | tf_op jit(solution)/shard_map/all_gather | solution.py:20
  177.5 8.5 %gather_fusion.1 = bf16[16,2048,64]{1,2,0:T(8,128)(2,1)} fusion(bf16[64,2048,64]{1,2,0:T(8,128)(2,1)} %all-gather.6.cloned.1.call-done, s32[1024]{0:T(1024)S(1)} %pad_clamp_fusion), kind=kCustom, calls=%fused_computation.1 | custom fusion | bytes 8388672 | tf_op jit(solution)/shard_map/gather | solution.py:24
  186.0 0.0 copy-done.2
  186.0 4.0 %convolution_bitcast_fusion = f32[16,32,64]{2,1,0:T(8,128)S(1)} fusion(bf16[16,2048,64]{1,2,0:T(8,128)(2,1)} %gather_fusion.1, bf16[16,32,2048]{2,1,0:T(8,128)(2,1)S(1)} %bitcast.13), kind=kOutput, calls=%fused_computation.6 | convolution fusion | flops 134217728 | bytes 6422528 | tf_op jit(solution)/shard_map/zlc,zcx->zlx/dot_general | solution.py:27
  190.0 38.9 %all-reduce.1 = bf16[16,32,64]{2,1,0:T(8,128)(2,1)S(1)} all-reduce(f32[16,32,64]{2,1,0:T(8,128)S(1)} %convolution_bitcast_fusion), channel_id=1, replica_groups=mesh['groups'=2,'replica'=4,'tensor'=4] {'tensor'}, use_global_device_ids=true, to_apply=%region_0.1 | all-reduce | flops 32768 | bytes 196608 | tf_op jit(solution)/shard_map/psum | solution.py:30
  228.9 2.0 convolution_multiply_fusion
  231.0 106.0 %all-gather.4.cloned.1.call-done = bf16[512,8192]{1,0:T(8,128)(2,1)} async-done(((bf16[512,2048]{1,0:T(8,128)(2,1)}), bf16[512,8192]{1,0:T(8,128)(2,1)}) %all-gather.4.cloned.1.call-update) | async-done | bytes 8388624 | tf_op jit(solution)/shard_map/all_gather | solution.py:12
  337.0 15.8 %fusion = bf16[512,1024]{1,0:T(8,128)(2,1)} fusion(f32[16,32,1024]{2,1,0:T(8,128)S(1)} %convolution_multiply_fusion, bf16[512,8192]{1,0:T(8,128)(2,1)} %all-gather.4.cloned.1.call-done, bf16[8192,1024]{1,0:T(8,128)(2,1)} %param.8), kind=kOutput, calls=%fused_computation.4 | convolution fusion | flops 8590983168 | bytes 28311552 | tf_op jit(solution)/shard_map/dot_general | solution.py:11
  352.8 0.0 copy-done.1
  (6 shorter events, 0.0 us)
Async XLA Ops:
  6.5 2.3 copy-start
  6.5 2.2 copy-start.4
  6.5 3.0 copy-start.3
  6.5 63.4 %all-gather.8.cloned.1.call-start = ((), (), s32[]{:S(2)}) async-start(), calls=%async_computation.2 | async-start | bytes 10485760 | tf_op jit(solution)/shard_map/all_gather | solution.py:21
  7.3 170.2 %all-gather.6.cloned.1.call-start = ((), (), s32[]{:S(2)}) async-start(), calls=%async_computation.1 | async-start | bytes 20971520 | tf_op jit(solution)/shard_map/all_gather | solution.py:20
  8.0 329.0 %all-gather.4.cloned.1.call-start = ((), (), s32[]{:S(2)}) async-start(), calls=%async_computation | async-start | bytes 10485760 | tf_op jit(solution)/shard_map/all_gather | solution.py:12
  75.3 110.7 %copy-start.2 = (bf16[512,2048]{1,0:T(8,128)(2,1)S(1)}, bf16[512,2048]{1,0:T(8,128)(2,1)}, u32[]{:S(2)}) copy-start(bf16[512,2048]{1,0:T(8,128)(2,1)} %param.7) | copy-start | bytes 6291460
  337.0 15.8 %copy-start.1 = (s32[4,4,2]{1,2,0:T(2,128)S(1)}, s32[4,4,2]{1,2,0:T(2,128)}, u32[]{:S(2)}) copy-start(s32[4,4,2]{1,2,0:T(2,128)} %param.11) | copy-start | bytes 388
Sparse Core Ops, SparseCore 0:
  8.9 60.9 all-gather.7
  71.5 105.9 all-gather.5
  179.0 157.9 all-gather.3
where the time goes:
time: 360 us; the launch traced here: 359 us
  waiting for transfers between devices  271 us (75%)
  blocking collectives  38.9 us (11%)
  matrix products  21.8 us (6%)
  local copies, waits for them, and re-layouts  14.7 us (4%)
  between operations  13.2 us (4%)
    all_gather x1, waiting for transfers between devices, shards(): lax.all_gather(tokens, 'tensor', axis=1, tiled=True)  106 us
    all_gather x1, waiting for transfers between devices, shards(): lax.all_gather(adapter_down, 'replica', axis=0, tiled=True)  102 us
    all_gather x1, waiting for transfers between devices, shards(): lax.all_gather(adapter_up, 'replica', axis=0, tiled=True)  60.3 us
    psum x1, blocking collectives, shards(): shrink_round = lax.psum(partial_shrink, 'tensor').astype(jnp.bfloat16)  38.9 us
    dot_general x1, matrix products, shards(): jnp.dot(lax.all_gather(tokens, 'tensor', axis=1, tiled=True), query_weigh...  15.8 us
    gather x1, local copies, waits for them, and re-layouts, shards(): down_weight_selected = down_weight_all[adapter]  8.54 us
  transfers between devices with their start and end apart: 3, of which 3 were waited for; matrix products, arithmetic and copies ran while one was open for 6% of the time, Pallas kernels for 0%

commit v1 on v0

v1 whole, which is shorter than its diff:
```python
import jax
import jax.numpy as jnp
from jax import lax
from jax.sharding import PartitionSpec as P

CHUNKS = 4


def exchange_adapters(adapter_down, adapter_up, send_table):
    me = lax.axis_index("replica")
    count = lax.axis_size("replica")
    downs, ups = [], []
    for k in range(count):
        wanted = send_table[me, me ^ k]
        down = adapter_down[wanted]
        up = adapter_up[wanted]
        if k:
            perm = [(i, i ^ k) for i in range(count)]
            down = lax.ppermute(down, "replica", perm)
            up = lax.ppermute(up, "replica", perm)
        downs.append(down)
        ups.append(up)
    return downs, ups


def adapter_term(tokens, adapter_down, adapter_up, send_table, block_slot, live_block_rows):
    count = live_block_rows.shape[0]
    block_rows = tokens.shape[0] // count
    slots_each = send_table.shape[2]
    rank = adapter_down.shape[2]
    me = lax.axis_index("replica")
    downs, ups = exchange_adapters(adapter_down, adapter_up, send_table)
    place = ((block_slot // slots_each) ^ me) * slots_each + block_slot % slots_each
    row_place = jnp.repeat(place, block_rows)
    partial = jnp.zeros((tokens.shape[0], rank), jnp.float32)
    for k, down in enumerate(downs):
        product = jnp.einsum("rd,cdx->rcx", tokens, down, preferred_element_type=jnp.float32)
        for c in range(slots_each):
            partial = jnp.where((row_place == k * slots_each + c)[:, None], product[:, c], partial)
    shrink_round = lax.psum(partial, "tensor").astype(jnp.bfloat16)
    live = jnp.arange(block_rows, dtype=jnp.int32)[None, :] < live_block_rows[:, None]
    live = live.reshape(-1)
    pieces = len(downs) * slots_each
    spread = jnp.where(
        (live[:, None] & (row_place[:, None] == jnp.arange(pieces, dtype=jnp.int32)[None, :]))[:, :, None],
        shrink_round[:, None, :],
        jnp.bfloat16(0),
    ).reshape(tokens.shape[0], pieces * rank)
    up_all = jnp.concatenate(ups, axis=0).reshape(pieces * rank, -1)
    return jnp.dot(spread, up_all, preferred_element_type=jnp.float32)


def shards_any(tokens, query_weight, adapter_down, adapter_up, send_table, block_slot, live_block_rows):
    delta = adapter_term(tokens, adapter_down, adapter_up, send_table, block_slot, live_block_rows)
    base = jnp.dot(
        lax.all_gather(tokens, "tensor", axis=1, tiled=True),
        query_weight,
        preferred_element_type=jnp.float32,
    )
    return (base + delta).astype(jnp.bfloat16)


def dot(a, b):
    return jnp.dot(a, b, preferred_element_type=jnp.float32)


def shards_line4(tokens, query_weight, adapter_down, adapter_up, send_table, block_slot, live_block_rows):
    t = lax.axis_index("tensor")
    rows, depth = tokens.shape
    step = rows // CHUNKS
    right = [(0, 1), (1, 2), (2, 3)]
    left = [(1, 0), (2, 1), (3, 2)]
    swap = [(1, 2), (2, 1)]

    near_at = jnp.where(t < 2, 2, 1)
    far_at = jnp.where(t < 2, 3, 0)
    peers = lax.axis_size("groups") * lax.axis_size("replica")
    peer = lax.axis_index(("groups", "replica"))
    each = 2 * depth // peers
    half = peers // 2
    start = jnp.where(peer < half, near_at, far_at) * depth + (peer % half) * each
    piece = lax.dynamic_slice_in_dim(query_weight, start, each, 0)
    piece = lax.ppermute(piece, "tensor", [(0, 1), (3, 2)])
    help_weight = lax.all_gather(piece, ("groups", "replica"), axis=0, tiled=True)

    delta = adapter_term(tokens, adapter_down, adapter_up, send_table, block_slot, live_block_rows)

    def weight_rows(i):
        return lax.dynamic_slice_in_dim(query_weight, jnp.clip(i, 0, 3) * depth, depth, 0)

    own_w = weight_rows(t)
    left_w = weight_rows(t - 1)
    right_w = weight_rows(t + 1)
    distant_w = weight_rows(jnp.where(t < 2, t + 2, t - 2))

    outs = []
    for c in range(CHUNKS):
        mine = tokens[c * step : (c + 1) * step]
        from_left = lax.ppermute(mine, "tensor", right)
        from_right = lax.ppermute(mine, "tensor", left)
        outer = jnp.where(t < 2, from_left, from_right)
        inner = jnp.where(t < 2, from_right, from_left)
        distant = lax.ppermute(outer, "tensor", swap)
        helped = dot(inner, help_weight[:depth]) + dot(distant, help_weight[depth:])
        helped = lax.ppermute(helped.astype(jnp.bfloat16), "tensor", [(1, 0), (2, 3)])
        total = dot(mine, own_w) + dot(from_left, left_w) + dot(from_right, right_w)
        total = total + dot(distant, distant_w) + delta[c * step : (c + 1) * step]
        outs.append((total + helped.astype(jnp.float32)).astype(jnp.bfloat16))
    return jnp.concatenate(outs, axis=0)


def solution(mesh):
    placed = (
        P(("groups", "replica"), "tensor"),
        P(None, "tensor"),
        P("replica", "tensor", None),
        P("replica", None, "tensor"),
        P("groups", None, None),
        P(("groups", "replica")),
        P(("groups", "replica")),
    )
    peers = mesh.shape["groups"] * mesh.shape["replica"]
    body = shards_line4 if mesh.shape["tensor"] == 4 and peers % 2 == 0 else shards_any
    return jax.shard_map(
        body,
        mesh=mesh,
        in_specs=placed,
        out_specs=P(("groups", "replica"), "tensor"),
        check_vma=False,
    )
```

time: 360 us -> 237 us (0.66)
  waiting for transfers between devices: 271 us -> 54.8 us
  matrix products: 21.8 us -> 66.1 us
  starting transfers between devices: 0.08 us -> 40.7 us
  local copies, waits for them, and re-layouts: 14.7 us -> 25.6 us
  blocking collectives: 38.9 us -> 30.1 us
  other arithmetic: 0.1 us -> 4.17 us
    all_gather x3 -> x1, waiting for transfers between devices: 268 us -> 0.01 us  [shards_line4(): lax.all_gather(piece, ('groups', 'replica'), axis=0, tiled=True)]
    ppermute x0 -> x23, waiting for transfers between devices: none -> 54.7 us  [the longest x4 29.5 us: shards_line4(): lax.ppermute(helped.astype(jnp.bfloat16), 'tensor', [(1, 0), (2, 3)])]
    dot_general x3 -> x29, matrix products: 21.8 us -> 66.1 us  [the longest x24 55.2 us: dot(): return jnp.dot(a, b, preferred_element_type=jnp.float32)]
    ppermute x0 -> x23, starting transfers between devices: none -> 40.7 us  [the longest x4 18.8 us: shards_line4(): from_left = lax.ppermute(mine, 'tensor', right)]
    psum x1, blocking collectives: 38.9 us -> 30.1 us  [adapter_term(): shrink_round = lax.psum(partial, 'tensor').astype(jnp.bfloat16)]
    gather x3 -> x8, local copies, waits for them, and re-layouts: 14.6 us -> 18.1 us  [the longest x4 13 us: exchange_adapters(): down = adapter_down[wanted]]
  transfers between devices with their start and end apart: 3 -> 24, of which waited for: 3 -> 8; matrix products, arithmetic and copies ran while one was open for 6% -> 35% of each run, Pallas kernels for 0% -> 0%
where the time goes in v1:
time: 237 us; the launch traced here: 236 us
  matrix products  66.1 us (28%)
  waiting for transfers between devices  54.8 us (23%)
  starting transfers between devices  40.7 us (17%)
  blocking collectives  30.1 us (13%)
  local copies, waits for them, and re-layouts  25.6 us (11%)
  between operations  14.3 us (6%)
  other arithmetic  4.17 us (2%)
    dot_general x24, matrix products, dot(): return jnp.dot(a, b, preferred_element_type=jnp.float32)  55.2 us
    psum x1, blocking collectives, adapter_term(): shrink_round = lax.psum(partial, 'tensor').astype(jnp.bfloat16)  30.1 us
    ppermute x4, waiting for transfers between devices, shards_line4(): lax.ppermute(helped.astype(jnp.bfloat16), 'tensor', [(1, 0), (2, 3)])  29.5 us
    ppermute x1, waiting for transfers between devices, shards_line4(): piece = lax.ppermute(piece, 'tensor', [(0, 1), (3, 2)])  22.3 us
    ppermute x4, starting transfers between devices, shards_line4(): from_left = lax.ppermute(mine, 'tensor', right)  18.8 us
    gather x4, local copies, waits for them, and re-layouts, exchange_adapters(): down = adapter_down[wanted]  13 us
    dot_general x4, matrix products, adapter_term(): jnp.einsum('rd,cdx->rcx', tokens, down, preferred_element_type=jnp.float32)  7.9 us
    ppermute x4, starting transfers between devices, shards_line4(): lax.ppermute(helped.astype(jnp.bfloat16), 'tensor', [(1, 0), (2, 3)])  6.05 us
  transfers between devices with their start and end apart: 24, of which 8 were waited for; matrix products, arithmetic and copies ran while one was open for 35% of the time, Pallas kernels for 0%

profile of v1, /device:TPU:0, one launch (start us, length us, event | category | flops | bytes accessed | tf_op | source)
XLA Modules:
  0.0 235.6 jit_solution(7306114087062491784)
XLA Ops:
  8.0 5.0 %collective-permute-start.9 = (bf16[512,1024]{1,0:T(8,128)(2,1)S(1)}, bf16[512,1024]{1,0:T(8,128)(2,1)S(1)}, u32[]{:S(2)}, u32[]{:S(2)}) collective-permute-start(bf16[512,1024]{1,0:T(8,128)(2,1)S(1)} %constant_dynamic-slice_fusion), channel_id=1, source_target_pairs={{0,1},{3,2},{4,5},{7,6},{8,9},{11,10},{12,13},{15,14},{16,17},{19,... | collective-permute-start | bytes 3145736 | tf_op jit(solution)/shard_map/ppermute | solution.py:83
  13.0 22.3 %collective-permute-done.9 = bf16[512,1024]{1,0:T(8,128)(2,1)S(1)} collective-permute-done((bf16[512,1024]{1,0:T(8,128)(2,1)S(1)}, bf16[512,1024]{1,0:T(8,128)(2,1)S(1)}, u32[]{:S(2)}, u32[]{:S(2)}) %collective-permute-start.9) | collective-permute-done | bytes 1048608 | tf_op jit(solution)/shard_map/ppermute | solution.py:83
  39.2 5.2 %collective-permute-start = (bf16[128,2048]{1,0:T(8,128)(2,1)}, bf16[128,2048]{1,0:T(8,128)(2,1)}, u32[]{:S(2)}, u32[]{:S(2)}) collective-permute-start(bf16[128,2048]{1,0:T(8,128)(2,1)} %get-tuple-element.9), channel_id=1, source_target_pairs={{0,1},{1,2},{2,3},{4,5},{5,6},{6,7},{8,9},{9,10},{10,11},{12,13},{... | collective-permute-start | bytes 1572872 | tf_op jit(solution)/shard_map/ppermute | solution.py:99
  46.0 3.9 %gather_fusion = bf16[2,2048,64]{1,2,0:T(8,128)(2,1)} fusion(bf16[16,2048,64]{1,2,0:T(8,128)(2,1)} %param.9, s32[1024]{0:T(1024)S(1)} %pad_clamp_fusion.3), kind=kCustom, calls=%fused_computation | custom fusion | bytes 1048584 | tf_op jit(solution)/shard_map/gather | solution.py:15
  54.3 3.6 %gather_fusion.2 = bf16[2,2048,64]{1,2,0:T(8,128)(2,1)} fusion(bf16[16,2048,64]{1,2,0:T(8,128)(2,1)} %param.9, s32[1024]{0:T(1024)S(1)} %pad_clamp_fusion.1), kind=kCustom, calls=%fused_computation.2 | custom fusion | bytes 1048584 | tf_op jit(solution)/shard_map/gather | solution.py:15
  61.1 4.0 %fusion.40 = f32[1024,128]{0,1:T(8,128)} fusion(bf16[8192,1024]{1,0:T(8,128)(2,1)} %param.8, s32[]{:T(128)S(6)} %select_n.172, bf16[512,2048]{1,0:T(8,128)(2,1)} %param.7), kind=kOutput, calls=%fused_computation.48 | convolution fusion | flops 536870912 | bytes 5242884 | tf_op jit(solution)/shard_map/dot_general | solution.py:64
  65.1 3.8 %fusion.42 = f32[1024,128]{0,1:T(8,128)} fusion(bf16[8192,1024]{1,0:T(8,128)(2,1)} %param.8, s32[]{:T(128)S(6)} %select_n.172, bf16[512,2048]{1,0:T(8,128)(2,1)S(1)} %copy-done.2), kind=kOutput, calls=%fused_computation.50 | convolution fusion | flops 536870912 | bytes 5242884 | tf_op jit(solution)/shard_map/dot_general | solution.py:64
  68.9 3.8 %fusion.44 = f32[1024,128]{0,1:T(8,128)} fusion(bf16[8192,1024]{1,0:T(8,128)(2,1)} %param.8, s32[]{:T(128)S(6)} %select_n.172, bf16[512,2048]{1,0:T(8,128)(2,1)S(1)} %copy-done.2), kind=kOutput, calls=%fused_computation.52 | convolution fusion | flops 536870912 | bytes 5242884 | tf_op jit(solution)/shard_map/dot_general | solution.py:64
  72.7 3.7 %fusion.46 = f32[1024,128]{0,1:T(8,128)} fusion(bf16[8192,1024]{1,0:T(8,128)(2,1)} %param.8, s32[]{:T(128)S(6)} %select_n.172, bf16[512,2048]{1,0:T(8,128)(2,1)S(1)} %copy-done.2), kind=kOutput, calls=%fused_computation.54 | convolution fusion | flops 536870912 | bytes 5242884 | tf_op jit(solution)/shard_map/dot_general | solution.py:64
  82.5 4.5 %collective-permute-start.11 = (bf16[128,2048]{1,0:T(8,128)(2,1)}, bf16[128,2048]{1,0:T(8,128)(2,1)S(1)}, u32[]{:S(2)}, u32[]{:S(2)}) collective-permute-start(bf16[128,2048]{1,0:T(8,128)(2,1)} %get-tuple-element.10), channel_id=1, source_target_pairs={{0,1},{1,2},{2,3},{4,5},{5,6},{6,7},{8,9},{9,10},{10,11},{12,13},{... | collective-permute-start | bytes 1572872 | tf_op jit(solution)/shard_map/ppermute | solution.py:99
  93.9 4.6 %collective-permute-start.15 = (bf16[128,2048]{1,0:T(8,128)(2,1)}, bf16[128,2048]{1,0:T(8,128)(2,1)S(1)}, u32[]{:S(2)}, u32[]{:S(2)}) collective-permute-start(bf16[128,2048]{1,0:T(8,128)(2,1)} %get-tuple-element.12), channel_id=1, source_target_pairs={{0,1},{1,2},{2,3},{4,5},{5,6},{6,7},{8,9},{9,10},{10,11},{12,13},{... | collective-permute-start | bytes 1572872 | tf_op jit(solution)/shard_map/ppermute | solution.py:99
  101.8 4.6 %collective-permute-start.19 = (bf16[128,2048]{1,0:T(8,128)(2,1)}, bf16[128,2048]{1,0:T(8,128)(2,1)S(1)}, u32[]{:S(2)}, u32[]{:S(2)}) collective-permute-start(bf16[128,2048]{1,0:T(8,128)(2,1)} %get-tuple-element.11), channel_id=1, source_target_pairs={{0,1},{1,2},{2,3},{4,5},{5,6},{6,7},{8,9},{9,10},{10,11},{12,13},{... | collective-permute-start | bytes 1572872 | tf_op jit(solution)/shard_map/ppermute | solution.py:99
  111.3 30.1 %all-reduce.1 = bf16[512,64]{0,1:T(8,128)(2,1)S(1)} all-reduce(f32[512,64]{0,1:T(8,128)S(1)} %fusion.202), channel_id=1, replica_groups=mesh['groups'=2,'replica'=4,'tensor'=4] {'tensor'}, use_global_device_ids=true, to_apply=%region_0.1 | all-reduce | flops 32768 | bytes 196608 | tf_op jit(solution)/shard_map/psum | solution.py:40
  143.6 4.0 %fusion.24 = f32[1024,128]{0,1:T(8,128)} fusion(bf16[128,2048]{1,0:T(8,128)(2,1)} %collective-permute-done.1, bf16[8192,1024]{1,0:T(8,128)(2,1)} %param.8, s32[]{:T(128)S(6)} %select_n.174), kind=kOutput, calls=%fused_computation.32 | convolution fusion | flops 536870912 | bytes 5242884 | tf_op jit(solution)/shard_map/dot_general | solution.py:64
  154.9 3.7 %fusion.26 = f32[1024,128]{0,1:T(8,128)} fusion(bf16[128,2048]{1,0:T(8,128)(2,1)S(1)} %copy-done.7, bf16[8192,1024]{1,0:T(8,128)(2,1)} %param.8, s32[]{:T(128)S(6)} %select_n.174), kind=kOutput, calls=%fused_computation.34 | convolution fusion | flops 536870912 | bytes 5242884 | tf_op jit(solution)/shard_map/dot_general | solution.py:64
  158.6 3.9 %fusion.28 = f32[1024,128]{0,1:T(8,128)} fusion(bf16[128,2048]{1,0:T(8,128)(2,1)S(1)} %collective-permute-done.16, bf16[8192,1024]{1,0:T(8,128)(2,1)} %param.8, s32[]{:T(128)S(6)} %select_n.174), kind=kOutput, calls=%fused_computation.36 | convolution fusion | flops 536870912 | bytes 5242884 | tf_op jit(solution)/shard_map/dot_general | solution.py:64
  162.5 3.9 %fusion.30 = f32[1024,128]{0,1:T(8,128)} fusion(bf16[128,2048]{1,0:T(8,128)(2,1)S(1)} %collective-permute-done.20, bf16[8192,1024]{1,0:T(8,128)(2,1)} %param.8, s32[]{:T(128)S(6)} %select_n.174), kind=kOutput, calls=%fused_computation.38 | convolution fusion | flops 536870912 | bytes 5242884 | tf_op jit(solution)/shard_map/dot_general | solution.py:64
  166.4 3.9 %fusion.22 = f32[128,1024]{1,0:T(8,128)} fusion(bf16[128,2048]{1,0:T(8,128)(2,1)S(1)} %collective-permute-done.2, bf16[8192,1024]{1,0:T(8,128)(2,1)} %param.8, s32[]{:T(128)S(6)} %select_n.178), kind=kOutput, calls=%fused_computation.30 | convolution fusion | flops 536870912 | bytes 5242884 | tf_op jit(solution)/shard_map/dot_general | solution.py:64
  175.7 3.2 %fusion.6 = f32[128,1024]{1,0:T(8,128)S(1)} fusion(bf16[128,2048]{1,0:T(8,128)(2,1)} %copy-done.26, bf16[4096,1024]{1,0:T(8,128)(2,1)} %all-gather.2.cloned.1.call-done), kind=kOutput, calls=%fused_computation.14 | convolution fusion | flops 536870912 | bytes 5242880 | tf_op jit(solution)/shard_map/dot_general | solution.py:64
  178.9 3.7 %fusion.149 = bf16[128,1024]{1,0:T(8,128)(2,1)S(1)} fusion(f32[128,1024]{1,0:T(8,128)S(1)} %fusion.6, bf16[4096,1024]{1,0:T(8,128)(2,1)} %all-gather.2.cloned.1.call-done, bf16[128,2048]{1,0:T(8,128)(2,1)} %collective-permute-done.1, bf16[128,2048]{1,0:T(8,128)(2,1)} %collective-permute-done, pred[]{:T(512)S(6)} %lt.126), kind=kOutput, calls=%fused_computation.96 | convolution fusion | flops 537395200 | bytes 6029313 | tf_op jit(solution)/shard_map/dot_general | solution.py:64
  193.5 16.9 %collective-permute-done.10 = bf16[128,1024]{1,0:T(8,128)(2,1)S(1)} collective-permute-done((bf16[128,1024]{1,0:T(8,128)(2,1)S(1)}, bf16[128,1024]{1,0:T(8,128)(2,1)S(1)}, u32[]{:S(2)}, u32[]{:S(2)}) %collective-permute-start.10) | collective-permute-done | bytes 262176 | tf_op jit(solution)/shard_map/ppermute | solution.py:105
  212.4 3.6 %collective-permute-done.14 = bf16[128,1024]{1,0:T(8,128)(2,1)S(1)} collective-permute-done((bf16[128,1024]{1,0:T(8,128)(2,1)S(1)}, bf16[128,1024]{1,0:T(8,128)(2,1)S(1)}, u32[]{:S(2)}, u32[]{:S(2)}) %collective-permute-start.14) | collective-permute-done | bytes 262176 | tf_op jit(solution)/shard_map/ppermute | solution.py:105
  216.9 4.7 %collective-permute-done.18 = bf16[128,1024]{1,0:T(8,128)(2,1)S(1)} collective-permute-done((bf16[128,1024]{1,0:T(8,128)(2,1)S(1)}, bf16[128,1024]{1,0:T(8,128)(2,1)S(1)}, u32[]{:S(2)}, u32[]{:S(2)}) %collective-permute-start.18) | collective-permute-done | bytes 262176 | tf_op jit(solution)/shard_map/ppermute | solution.py:105
  222.5 4.3 %collective-permute-done.22 = bf16[128,1024]{1,0:T(8,128)(2,1)S(1)} collective-permute-done((bf16[128,1024]{1,0:T(8,128)(2,1)S(1)}, bf16[128,1024]{1,0:T(8,128)(2,1)S(1)}, u32[]{:S(2)}, u32[]{:S(2)}) %collective-permute-start.22) | collective-permute-done | bytes 262176 | tf_op jit(solution)/shard_map/ppermute | solution.py:105
  (171 shorter events, 66.7 us)
Async XLA Ops:
  6.5 169.2 %all-gather.2.cloned.1.call-start = ((), (), s32[]{:S(2)}) async-start(), calls=%async_computation | async-start | bytes 9437184 | tf_op jit(solution)/shard_map/all_gather | solution.py:84
  8.0 27.3 %collective-permute-start.9 = (bf16[512,1024]{1,0:T(8,128)(2,1)S(1)}, bf16[512,1024]{1,0:T(8,128)(2,1)S(1)}, u32[]{:S(2)}, u32[]{:S(2)}) collective-permute-start(bf16[512,1024]{1,0:T(8,128)(2,1)S(1)} %constant_dynamic-slice_fusion), channel_id=1, source_target_pairs={{0,1},{3,2},{4,5},{7,6},{8,9},{11,10},{12,13},{15,14},{16,17},{19,... | collective-permute-start | bytes 3145736 | tf_op jit(solution)/shard_map/ppermute | solution.py:83
  39.2 61.2 %collective-permute-start = (bf16[128,2048]{1,0:T(8,128)(2,1)}, bf16[128,2048]{1,0:T(8,128)(2,1)}, u32[]{:S(2)}, u32[]{:S(2)}) collective-permute-start(bf16[128,2048]{1,0:T(8,128)(2,1)} %get-tuple-element.9), channel_id=1, source_target_pairs={{0,1},{1,2},{2,3},{4,5},{5,6},{6,7},{8,9},{9,10},{10,11},{12,13},{... | collective-permute-start | bytes 1572872 | tf_op jit(solution)/shard_map/ppermute | solution.py:99
  44.4 57.4 %collective-permute-start.1 = (bf16[128,2048]{1,0:T(8,128)(2,1)}, bf16[128,2048]{1,0:T(8,128)(2,1)}, u32[]{:S(2)}, u32[]{:S(2)}) collective-permute-start(bf16[128,2048]{1,0:T(8,128)(2,1)} %get-tuple-element.9), channel_id=1, source_target_pairs={{1,0},{2,1},{3,2},{5,4},{6,5},{7,6},{9,8},{10,9},{11,10},{13,12},{... | collective-permute-start | bytes 1572872 | tf_op jit(solution)/shard_map/ppermute | solution.py:100
  49.9 32.7 %collective-permute-start.3 = (bf16[2,2048,64]{1,2,0:T(8,128)(2,1)}, bf16[2,2048,64]{1,2,0:T(8,128)(2,1)}, u32[]{:S(2)}, u32[]{:S(2)}) collective-permute-start(bf16[2,2048,64]{1,2,0:T(8,128)(2,1)} %gather_fusion), channel_id=1, source_target_pairs={{0,12},{4,8},{8,4},{12,0},{1,13},{5,9},{9,5},{13,1},{2,14},{6,10},... | collective-permute-start | bytes 1572872 | tf_op jit(solution)/shard_map/ppermute | solution.py:19
  52.7 37.3 %collective-permute-start.4 = (bf16[2,2048,64]{1,2,0:T(8,128)(2,1)S(1)}, bf16[2,2048,64]{1,2,0:T(8,128)(2,1)}, u32[]{:S(2)}, u32[]{:S(2)}) collective-permute-start(bf16[2,2048,64]{1,2,0:T(8,128)(2,1)S(1)} %gather_fusion.1), channel_id=1, source_target_pairs={{0,8},{4,12},{8,0},{12,4},{1,9},{5,13},{9,1},{13,5},{2,10},{6,14},... | collective-permute-start | bytes 1572872 | tf_op jit(solution)/shard_map/ppermute | solution.py:19
  57.9 36.0 %collective-permute-start.5 = (bf16[2,2048,64]{1,2,0:T(8,128)(2,1)}, bf16[2,2048,64]{1,2,0:T(8,128)(2,1)}, u32[]{:S(2)}, u32[]{:S(2)}) collective-permute-start(bf16[2,2048,64]{1,2,0:T(8,128)(2,1)} %gather_fusion.2), channel_id=1, source_target_pairs={{0,4},{4,0},{8,12},{12,8},{1,5},{5,1},{9,13},{13,9},{2,6},{6,2},{1... | collective-permute-start | bytes 1572872 | tf_op jit(solution)/shard_map/ppermute | solution.py:19
  82.5 25.8 %collective-permute-start.11 = (bf16[128,2048]{1,0:T(8,128)(2,1)}, bf16[128,2048]{1,0:T(8,128)(2,1)S(1)}, u32[]{:S(2)}, u32[]{:S(2)}) collective-permute-start(bf16[128,2048]{1,0:T(8,128)(2,1)} %get-tuple-element.10), channel_id=1, source_target_pairs={{0,1},{1,2},{2,3},{4,5},{5,6},{6,7},{8,9},{9,10},{10,11},{12,13},{... | collective-permute-start | bytes 1572872 | tf_op jit(solution)/shard_map/ppermute | solution.py:99
  90.0 19.6 %collective-permute-start.12 = (bf16[128,2048]{1,0:T(8,128)(2,1)}, bf16[128,2048]{1,0:T(8,128)(2,1)S(1)}, u32[]{:S(2)}, u32[]{:S(2)}) collective-permute-start(bf16[128,2048]{1,0:T(8,128)(2,1)} %get-tuple-element.10), channel_id=1, source_target_pairs={{1,0},{2,1},{3,2},{5,4},{6,5},{7,6},{9,8},{10,9},{11,10},{13,12},{... | collective-permute-start | bytes 1572872 | tf_op jit(solution)/shard_map/ppermute | solution.py:100
  93.9 47.5 %collective-permute-start.15 = (bf16[128,2048]{1,0:T(8,128)(2,1)}, bf16[128,2048]{1,0:T(8,128)(2,1)S(1)}, u32[]{:S(2)}, u32[]{:S(2)}) collective-permute-start(bf16[128,2048]{1,0:T(8,128)(2,1)} %get-tuple-element.12), channel_id=1, source_target_pairs={{0,1},{1,2},{2,3},{4,5},{5,6},{6,7},{8,9},{9,10},{10,11},{12,13},{... | collective-permute-start | bytes 1572872 | tf_op jit(solution)/shard_map/ppermute | solution.py:99
  100.5 41.6 %collective-permute-start.16 = (bf16[128,2048]{1,0:T(8,128)(2,1)}, bf16[128,2048]{1,0:T(8,128)(2,1)S(1)}, u32[]{:S(2)}, u32[]{:S(2)}) collective-permute-start(bf16[128,2048]{1,0:T(8,128)(2,1)} %get-tuple-element.12), channel_id=1, source_target_pairs={{1,0},{2,1},{3,2},{5,4},{6,5},{7,6},{9,8},{10,9},{11,10},{13,12},{... | collective-permute-start | bytes 1572872 | tf_op jit(solution)/shard_map/ppermute | solution.py:100
  101.8 40.3 %collective-permute-start.19 = (bf16[128,2048]{1,0:T(8,128)(2,1)}, bf16[128,2048]{1,0:T(8,128)(2,1)S(1)}, u32[]{:S(2)}, u32[]{:S(2)}) collective-permute-start(bf16[128,2048]{1,0:T(8,128)(2,1)} %get-tuple-element.11), channel_id=1, source_target_pairs={{0,1},{1,2},{2,3},{4,5},{5,6},{6,7},{8,9},{9,10},{10,11},{12,13},{... | collective-permute-start | bytes 1572872 | tf_op jit(solution)/shard_map/ppermute | solution.py:99
  108.3 34.6 %collective-permute-start.20 = (bf16[128,2048]{1,0:T(8,128)(2,1)}, bf16[128,2048]{1,0:T(8,128)(2,1)S(1)}, u32[]{:S(2)}, u32[]{:S(2)}) collective-permute-start(bf16[128,2048]{1,0:T(8,128)(2,1)} %get-tuple-element.11), channel_id=1, source_target_pairs={{1,0},{2,1},{3,2},{5,4},{6,5},{7,6},{9,8},{10,9},{11,10},{13,12},{... | collective-permute-start | bytes 1572872 | tf_op jit(solution)/shard_map/ppermute | solution.py:100
  109.6 38.1 %collective-permute-start.6 = (bf16[2,64,1024]{2,1,0:T(8,128)(2,1)}, bf16[2,64,1024]{2,1,0:T(8,128)(2,1)}, u32[]{:S(2)}, u32[]{:S(2)}) collective-permute-start(bf16[2,64,1024]{2,1,0:T(8,128)(2,1)} %gather_fusion.5), channel_id=1, source_target_pairs={{0,4},{4,0},{8,12},{12,8},{1,5},{5,1},{9,13},{13,9},{2,6},{6,2},{1... | collective-permute-start | bytes 786440 | tf_op jit(solution)/shard_map/ppermute | solution.py:20
  141.4 9.4 %collective-permute-start.7 = (bf16[2,64,1024]{2,1,0:T(8,128)(2,1)}, bf16[2,64,1024]{2,1,0:T(8,128)(2,1)S(1)}, u32[]{:S(2)}, u32[]{:S(2)}) collective-permute-start(bf16[2,64,1024]{2,1,0:T(8,128)(2,1)} %gather_fusion.6), channel_id=1, source_target_pairs={{0,8},{4,12},{8,0},{12,4},{1,9},{5,13},{9,1},{13,5},{2,10},{6,14},... | collective-permute-start | bytes 786440 | tf_op jit(solution)/shard_map/ppermute | solution.py:20
  142.1 9.8 %collective-permute-start.8 = (bf16[2,64,1024]{2,1,0:T(8,128)(2,1)}, bf16[2,64,1024]{2,1,0:T(8,128)(2,1)S(1)}, u32[]{:S(2)}, u32[]{:S(2)}) collective-permute-start(bf16[2,64,1024]{2,1,0:T(8,128)(2,1)} %gather_fusion.7), channel_id=1, source_target_pairs={{0,12},{4,8},{8,4},{12,0},{1,13},{5,9},{9,5},{13,1},{2,14},{6,10},... | collective-permute-start | bytes 786440 | tf_op jit(solution)/shard_map/ppermute | solution.py:20
  142.1 24.2 %collective-permute-start.2 = (bf16[128,2048]{1,0:T(8,128)(2,1)}, bf16[128,2048]{1,0:T(8,128)(2,1)S(1)}, u32[]{:S(2)}, u32[]{:S(2)}) collective-permute-start(bf16[128,2048]{1,0:T(8,128)(2,1)} %broadcast_select_fusion.3), channel_id=1, source_target_pairs={{1,2},{2,1},{5,6},{6,5},{9,10},{10,9},{13,14},{14,13},{17,18},{18,... | collective-permute-start | bytes 1572872 | tf_op jit(solution)/shard_map/ppermute | solution.py:103
  142.9 27.4 %collective-permute-start.13 = (bf16[128,2048]{1,0:T(8,128)(2,1)}, bf16[128,2048]{1,0:T(8,128)(2,1)S(1)}, u32[]{:S(2)}, u32[]{:S(2)}) collective-permute-start(bf16[128,2048]{1,0:T(8,128)(2,1)} %broadcast_select_fusion.2), channel_id=1, source_target_pairs={{1,2},{2,1},{5,6},{6,5},{9,10},{10,9},{13,14},{14,13},{17,18},{18,... | collective-permute-start | bytes 1572872 | tf_op jit(solution)/shard_map/ppermute | solution.py:103
  147.7 24.2 %collective-permute-start.17 = (bf16[128,2048]{1,0:T(8,128)(2,1)S(1)}, bf16[128,2048]{1,0:T(8,128)(2,1)S(1)}, u32[]{:S(2)}, u32[]{:S(2)}) collective-permute-start(bf16[128,2048]{1,0:T(8,128)(2,1)S(1)} %broadcast_select_fusion.1), channel_id=1, source_target_pairs={{1,2},{2,1},{5,6},{6,5},{9,10},{10,9},{13,14},{14,13},{17,18},{18,... | collective-permute-start | bytes 1572872 | tf_op jit(solution)/shard_map/ppermute | solution.py:103
  150.8 22.6 %collective-permute-start.21 = (bf16[128,2048]{1,0:T(8,128)(2,1)S(1)}, bf16[128,2048]{1,0:T(8,128)(2,1)S(1)}, u32[]{:S(2)}, u32[]{:S(2)}) collective-permute-start(bf16[128,2048]{1,0:T(8,128)(2,1)S(1)} %broadcast_select_fusion), channel_id=1, source_target_pairs={{1,2},{2,1},{5,6},{6,5},{9,10},{10,9},{13,14},{14,13},{17,18},{18,... | collective-permute-start | bytes 1572872 | tf_op jit(solution)/shard_map/ppermute | solution.py:103
  182.6 27.8 %collective-permute-start.10 = (bf16[128,1024]{1,0:T(8,128)(2,1)S(1)}, bf16[128,1024]{1,0:T(8,128)(2,1)S(1)}, u32[]{:S(2)}, u32[]{:S(2)}) collective-permute-start(bf16[128,1024]{1,0:T(8,128)(2,1)S(1)} %fusion.149), channel_id=1, source_target_pairs={{1,0},{2,3},{5,4},{6,7},{9,8},{10,11},{13,12},{14,15},{17,16},{18,... | collective-permute-start | bytes 786440 | tf_op jit(solution)/shard_map/ppermute | solution.py:105
  185.5 30.5 %collective-permute-start.14 = (bf16[128,1024]{1,0:T(8,128)(2,1)S(1)}, bf16[128,1024]{1,0:T(8,128)(2,1)S(1)}, u32[]{:S(2)}, u32[]{:S(2)}) collective-permute-start(bf16[128,1024]{1,0:T(8,128)(2,1)S(1)} %fusion.146), channel_id=1, source_target_pairs={{1,0},{2,3},{5,4},{6,7},{9,8},{10,11},{13,12},{14,15},{17,16},{18,... | collective-permute-start | bytes 786440 | tf_op jit(solution)/shard_map/ppermute | solution.py:105
  188.6 33.0 %collective-permute-start.18 = (bf16[128,1024]{1,0:T(8,128)(2,1)S(1)}, bf16[128,1024]{1,0:T(8,128)(2,1)S(1)}, u32[]{:S(2)}, u32[]{:S(2)}) collective-permute-start(bf16[128,1024]{1,0:T(8,128)(2,1)S(1)} %fusion.143), channel_id=1, source_target_pairs={{1,0},{2,3},{5,4},{6,7},{9,8},{10,11},{13,12},{14,15},{17,16},{18,... | collective-permute-start | bytes 786440 | tf_op jit(solution)/shard_map/ppermute | solution.py:105
  191.8 35.0 %collective-permute-start.22 = (bf16[128,1024]{1,0:T(8,128)(2,1)S(1)}, bf16[128,1024]{1,0:T(8,128)(2,1)S(1)}, u32[]{:S(2)}, u32[]{:S(2)}) collective-permute-start(bf16[128,1024]{1,0:T(8,128)(2,1)S(1)} %fusion.140), channel_id=1, source_target_pairs={{1,0},{2,3},{5,4},{6,7},{9,8},{10,11},{13,12},{14,15},{17,16},{18,... | collective-permute-start | bytes 786440 | tf_op jit(solution)/shard_map/ppermute | solution.py:105
  (42 other events, 639.6 us)
Sparse Core Ops, SparseCore 0:
  36.4 69.4 all-gather.1

commit v2 on v1

v2 whole, which is shorter than its diff:
```python
import jax
import jax.numpy as jnp
from jax import lax
from jax.experimental import pallas as pl
from jax.experimental.pallas import tpu as pltpu
from jax.sharding import PartitionSpec as P

CHUNKS = 4
TILE = 256
MESH = pl.DeviceIdType.MESH

DOWN, UP, PIECE = 0, 3, 6
ALONG_X, ALONG_Y, MATE = 7, 8, 9
X_THEN_Y, Y_THEN_X = 10, 11
MATE_X, MATE_Y, MATE_D0, MATE_D1 = 12, 13, 14, 15
NEAR_END, NEAR_MID, SHRINK = 16, 17, 18
OUTER, FORWARD, HELPED = 21, 21 + CHUNKS, 21 + 2 * CHUNKS
COPIES = 21 + 3 * CHUNKS


def exchange_adapters(adapter_down, adapter_up, send_table):
    me = lax.axis_index("replica")
    count = lax.axis_size("replica")
    downs, ups = [], []
    for k in range(count):
        wanted = send_table[me, me ^ k]
        down = adapter_down[wanted]
        up = adapter_up[wanted]
        if k:
            perm = [(i, i ^ k) for i in range(count)]
            down = lax.ppermute(down, "replica", perm)
            up = lax.ppermute(up, "replica", perm)
        downs.append(down)
        ups.append(up)
    return downs, ups


def adapter_term(tokens, adapter_down, adapter_up, send_table, block_slot, live_block_rows):
    count = live_block_rows.shape[0]
    block_rows = tokens.shape[0] // count
    slots_each = send_table.shape[2]
    rank = adapter_down.shape[2]
    me = lax.axis_index("replica")
    downs, ups = exchange_adapters(adapter_down, adapter_up, send_table)
    place = ((block_slot // slots_each) ^ me) * slots_each + block_slot % slots_each
    row_place = jnp.repeat(place, block_rows)
    partial = jnp.zeros((tokens.shape[0], rank), jnp.float32)
    for k, down in enumerate(downs):
        product = jnp.einsum("rd,cdx->rcx", tokens, down, preferred_element_type=jnp.float32)
        for c in range(slots_each):
            partial = jnp.where((row_place == k * slots_each + c)[:, None], product[:, c], partial)
    shrink_round = lax.psum(partial, "tensor").astype(jnp.bfloat16)
    live = jnp.arange(block_rows, dtype=jnp.int32)[None, :] < live_block_rows[:, None]
    live = live.reshape(-1)
    pieces = len(downs) * slots_each
    spread = jnp.where(
        (live[:, None] & (row_place[:, None] == jnp.arange(pieces, dtype=jnp.int32)[None, :]))[:, :, None],
        shrink_round[:, None, :],
        jnp.bfloat16(0),
    ).reshape(tokens.shape[0], pieces * rank)
    up_all = jnp.concatenate(ups, axis=0).reshape(pieces * rank, -1)
    return jnp.dot(spread, up_all, preferred_element_type=jnp.float32)


def shards_any(tokens, query_weight, adapter_down, adapter_up, send_table, block_slot, live_block_rows):
    delta = adapter_term(tokens, adapter_down, adapter_up, send_table, block_slot, live_block_rows)
    base = jnp.dot(
        lax.all_gather(tokens, "tensor", axis=1, tiled=True),
        query_weight,
        preferred_element_type=jnp.float32,
    )
    return (base + delta).astype(jnp.bfloat16)


def line4_kernel(
    tokens, weight, down_send, up_send, code, out,
    w, help_w, own, near, outer, distant, acc, acc_h, h_send, h_recv, downs, ups, spread, shr,
    send, recv, local,
):
    g, r, t = lax.axis_index("groups"), lax.axis_index("replica"), lax.axis_index("tensor")
    rows, depth = own.shape
    step = rows // CHUNKS
    each = help_w.shape[0] // 8
    is_end = (t == 0) | (t == 3)
    is_mid = (t == 1) | (t == 2)
    inner = jnp.where(t < 2, t + 1, t - 1)
    edge = jnp.where(t < 2, 0, 3)
    other = 3 - t
    near_at = jnp.where(t < 2, 2, 1)
    far_at = jnp.where(t < 2, 3, 0)
    inner_at = jnp.where(is_end, inner, other)

    def remote(i, src, dst, **device_id):
        return pltpu.make_async_remote_copy(
            src_ref=src, dst_ref=dst, send_sem=send.at[i], recv_sem=recv.at[i],
            device_id=device_id, device_id_type=MESH,
        )

    def block(i):
        return pl.ds(pl.multiple_of(i * depth, depth), depth)

    def part(c):
        return pl.ds(c * step, step)

    def load_w(n, i):
        return pltpu.make_async_copy(weight.at[block(i)], w.at[block(i)], local.at[n])

    local_own = pltpu.make_async_copy(tokens, own, local.at[4])
    local_down = pltpu.make_async_copy(down_send.at[0], downs.at[0], local.at[5])
    local_up = pltpu.make_async_copy(up_send.at[0], ups.at[0], local.at[6])
    local_own.start()
    loads = [load_w(n, lax.rem(t + n, 4)) for n in range(4)]
    loads[0].start()

    barrier = pltpu.get_barrier_semaphore()
    for d in range(1, 4):
        pl.semaphore_signal(barrier, inc=1, device_id={"tensor": lax.rem(t + d, 4)}, device_id_type=MESH)
        pl.semaphore_signal(barrier, inc=1, device_id={"replica": r ^ d}, device_id_type=MESH)
    pl.semaphore_signal(barrier, inc=1, device_id={"groups": 1 - g}, device_id_type=MESH)
    pl.semaphore_wait(barrier, 7)

    peer = g * 4 + r

    def spot(p, half=None):
        if half is None:
            return help_w.at[pl.ds(pl.multiple_of(p * each, each), each)]
        return help_w.at[pl.ds(pl.multiple_of(p * each + half * (each // 2), each // 2), each // 2)]

    rx, gy, rc = r ^ 2, 1 - g, r ^ 1
    px, py, pd = g * 4 + rx, gy * 4 + r, gy * 4 + rx
    piece_row = jnp.where(g == 0, near_at, far_at) * depth + r * each
    piece = remote(
        PIECE, weight.at[pl.ds(pl.multiple_of(piece_row, each), each)], spot(peer), tensor=inner
    )
    along_x = remote(ALONG_X, spot(peer), spot(peer), replica=rx)
    along_y = remote(ALONG_Y, spot(peer), spot(peer), groups=gy)
    mate = remote(MATE, spot(peer), spot(peer), replica=rc)
    x_then_y = remote(X_THEN_Y, spot(px, 0), spot(px, 0), groups=gy)
    y_then_x = remote(Y_THEN_X, spot(py, 1), spot(py, 1), replica=rx)
    mate_x = remote(MATE_X, spot(px), spot(px), replica=rc)
    mate_y = remote(MATE_Y, spot(py), spot(py), replica=rc)
    mate_d0 = remote(MATE_D0, spot(pd, 0), spot(pd, 0), replica=rc)
    mate_d1 = remote(MATE_D1, spot(pd, 1), spot(pd, 1), replica=rc)
    near_end = remote(NEAR_END, tokens, near, tensor=edge)
    near_mid = remote(NEAR_MID, tokens, near, tensor=other)
    to_inner = [remote(OUTER + c, tokens.at[part(c)], outer.at[part(c)], tensor=inner) for c in range(CHUNKS)]
    forward = [remote(FORWARD + c, outer.at[part(c)], distant.at[part(c)], tensor=other) for c in range(CHUNKS)]
    helped = [remote(HELPED + c, h_send.at[part(c)], h_recv.at[part(c)], tensor=edge) for c in range(CHUNKS)]
    adapters = []
    for k in (2, 3, 1):
        adapters.append(remote(DOWN + k - 1, down_send.at[k], downs.at[k], replica=r ^ k))
        adapters.append(remote(UP + k - 1, up_send.at[k], ups.at[k], replica=r ^ k))
    shrinks = [
        remote(SHRINK + d - 1, shr.at[t], shr.at[t], tensor=lax.rem(t + d, 4)) for d in range(1, 4)
    ]

    def product(x, x_rows, weights, w_rows, put):
        def tile(n, carry):
            cols = pl.ds(pl.multiple_of(n * TILE, TILE), TILE)
            put(cols, jnp.dot(x[x_rows, :], weights[w_rows, cols], preferred_element_type=jnp.float32))
            return carry

        lax.fori_loop(0, w.shape[1] // TILE, tile, 0)

    everything = pl.ds(0, rows)

    def add_base(x, x_rows, i):
        def put(cols, value):
            acc[x_rows, cols] += value

        product(x, x_rows, w, block(i), put)

    def own_base():
        local_own.wait()
        loads[0].wait()

        def put(cols, value):
            acc[:, cols] = value

        product(own, everything, w, block(t), put)

    low = lax.broadcasted_iota(jnp.int32, (rows, 128), 1) < 64

    def shrink_send():
        for copy in adapters:
            copy.wait_recv()
        local_down.wait()
        total = jnp.zeros((rows, 128), jnp.float32)
        for k in range(4):
            value = jnp.dot(own[...], downs[k], preferred_element_type=jnp.float32)
            hit = code[...] == jnp.where(low, 2 * k, 2 * k + 1)
            total = total + jnp.where(hit, value, 0.0)
        both = total + pltpu.roll(total, 64, 1)
        half = rows // 2
        shr[t] = jnp.where(low[:half], both[:half], both[half:])
        for copy in shrinks:
            copy.start()

    def add_delta():
        for d in range(1, 4):
            from_t = lax.rem(t + 4 - d, 4)
            remote(SHRINK + d - 1, shr.at[from_t], shr.at[from_t], tensor=lax.rem(t + d, 4)).wait_recv()
        local_up.wait()
        total = (shr[0] + shr[1]) + (shr[2] + shr[3])
        turned = pltpu.roll(total, 64, 1)
        half = rows // 2
        top = low[:half]
        both = jnp.concatenate([jnp.where(top, total, turned), jnp.where(top, turned, total)], axis=0)
        for k in range(4):
            hit = code[...] == jnp.where(low, 2 * k, 2 * k + 1)
            spread[:, k * 128 : (k + 1) * 128] = jnp.where(hit, both, 0.0).astype(jnp.bfloat16)

        def tile(n, carry):
            cols = pl.ds(pl.multiple_of(n * TILE, TILE), TILE)
            value = jnp.zeros((rows, TILE), jnp.float32)
            for k in range(4):
                value = value + jnp.dot(
                    spread[:, k * 128 : (k + 1) * 128], ups[k, :, cols], preferred_element_type=jnp.float32
                )
            acc[:, cols] += value
            return carry

        lax.fori_loop(0, w.shape[1] // TILE, tile, 0)

    @pl.when(is_end)
    def _():
        piece.start()

    @pl.when(is_mid)
    def _():
        near_mid.start()
        near_end.start()

    for copy in adapters:
        copy.start()
    local_down.start()
    local_up.start()
    for load in loads[1:]:
        load.start()
    own_base()
    for load in loads[1:]:
        load.wait()

    @pl.when(is_end)
    def _():
        piece.wait_send()
        to_inner[0].start()
        to_inner[1].start()
        to_inner[0].wait_send()
        to_inner[2].start()
        to_inner[1].wait_send()
        to_inner[3].start()
        shrink_send()
        near_end.wait_recv()
        add_base(near, everything, inner_at)
        add_delta()
        for c in range(CHUNKS):
            helped[c].wait_recv()
            out[part(c), :] = (acc[part(c), :] + h_recv[part(c), :].astype(jnp.float32)).astype(out.dtype)
        to_inner[2].wait_send()
        to_inner[3].wait_send()

    @pl.when(is_mid)
    def _():
        piece.wait_recv()
        along_x.start()
        along_y.start()
        mate.start()
        to_inner[0].wait_recv()
        forward[0].start()
        remote(ALONG_X, spot(px), spot(px), replica=rx).wait_recv()
        x_then_y.start()
        mate_x.start()
        remote(ALONG_Y, spot(py), spot(py), groups=gy).wait_recv()
        y_then_x.start()
        mate_y.start()
        to_inner[1].wait_recv()
        forward[1].start()
        shrink_send()
        near_mid.wait_recv()
        add_base(near, everything, inner_at)
        to_inner[2].wait_recv()
        forward[2].start()
        remote(X_THEN_Y, spot(pd, 0), spot(pd, 0), groups=gy).wait_recv()
        mate_d0.start()
        remote(Y_THEN_X, spot(pd, 1), spot(pd, 1), replica=rx).wait_recv()
        mate_d1.start()
        to_inner[3].wait_recv()
        forward[3].start()
        add_base(outer, everything, edge)
        pc = g * 4 + rc
        remote(MATE, spot(pc), spot(pc), replica=rc).wait_recv()
        remote(MATE_X, spot(pc ^ 2), spot(pc ^ 2), replica=rc).wait_recv()
        remote(MATE_Y, spot(gy * 4 + rc), spot(gy * 4 + rc), replica=rc).wait_recv()
        qd = gy * 4 + (rc ^ 2)
        remote(MATE_D0, spot(qd, 0), spot(qd, 0), replica=rc).wait_recv()
        remote(MATE_D1, spot(qd, 1), spot(qd, 1), replica=rc).wait_recv()

        def put_near(cols, value):
            acc_h[:, cols] = value

        product(near, everything, help_w, pl.ds(0, depth), put_near)
        add_delta()
        for c in range(CHUNKS):
            forward[c].wait_recv()

            def put_far(cols, value):
                h_send[part(c), cols] = (acc_h[part(c), cols] + value).astype(jnp.bfloat16)

            product(distant, part(c), help_w, pl.ds(depth, depth), put_far)
            helped[c].start()
            add_base(distant, part(c), 3 - edge)
            out[part(c), :] = acc[part(c), :].astype(out.dtype)
        for copy in [near_mid, near_end, along_x, along_y, mate, x_then_y, y_then_x]:
            copy.wait_send()
        for copy in [mate_x, mate_y, mate_d0, mate_d1] + forward + helped:
            copy.wait_send()

    for copy in adapters + shrinks:
        copy.wait_send()


def shards_line4(tokens, query_weight, adapter_down, adapter_up, send_table, block_slot, live_block_rows):
    me = lax.axis_index("replica")
    rows, depth = tokens.shape
    cols = query_weight.shape[1]
    rank = adapter_down.shape[2]
    wanted = jnp.concatenate([send_table[me, me ^ k] for k in range(4)])
    down_send = adapter_down[wanted].reshape(4, 2, depth, rank).transpose(0, 2, 1, 3).reshape(4, depth, 2 * rank)
    up_send = adapter_up[wanted].reshape(4, 2 * rank, cols)
    count = block_slot.shape[0]
    place = ((block_slot // 2) ^ me) * 2 + block_slot % 2
    live = jnp.arange(rows // count, dtype=jnp.int32)[None, :] < live_block_rows[:, None]
    code = jnp.where(live, place[:, None], -1).reshape(rows, 1)
    code = jnp.broadcast_to(code, (rows, 128))
    bf16, f32 = jnp.bfloat16, jnp.float32
    any_space = pl.BlockSpec(memory_space=pl.ANY)
    vmem = pl.BlockSpec(memory_space=pltpu.VMEM)
    return pl.pallas_call(
        line4_kernel,
        out_shape=jax.ShapeDtypeStruct((rows, cols), bf16),
        in_specs=[any_space] * 4 + [vmem],
        out_specs=vmem,
        scratch_shapes=[
            pltpu.VMEM((4 * depth, cols), bf16),
            pltpu.VMEM((2 * depth, cols), bf16),
            pltpu.VMEM((rows, depth), bf16),
            pltpu.VMEM((rows, depth), bf16),
            pltpu.VMEM((rows, depth), bf16),
            pltpu.VMEM((rows, depth), bf16),
            pltpu.VMEM((rows, cols), f32),
            pltpu.VMEM((rows, cols), f32),
            pltpu.VMEM((rows, cols), bf16),
            pltpu.VMEM((rows, cols), bf16),
            pltpu.VMEM((4, depth, 2 * rank), bf16),
            pltpu.VMEM((4, 2 * rank, cols), bf16),
            pltpu.VMEM((rows, 8 * rank), bf16),
            pltpu.VMEM((4, rows // 2, 128), f32),
            pltpu.SemaphoreType.DMA((COPIES,)),
            pltpu.SemaphoreType.DMA((COPIES,)),
            pltpu.SemaphoreType.DMA((7,)),
        ],
        compiler_params=pltpu.CompilerParams(
            collective_id=0, has_side_effects=True, vmem_limit_bytes=56 << 20
        ),
        cost_estimate=pl.CostEstimate(flops=13 * 10**9, bytes_accessed=40 << 20, transcendentals=0),
    )(tokens, query_weight, down_send, up_send, code)


def solution(mesh):
    placed = (
        P(("groups", "replica"), "tensor"),
        P(None, "tensor"),
        P("replica", "tensor", None),
        P("replica", None, "tensor"),
        P("groups", None, None),
        P(("groups", "replica")),
        P(("groups", "replica")),
    )
    sizes = (mesh.shape["groups"], mesh.shape["replica"], mesh.shape["tensor"])
    body = shards_line4 if sizes == (2, 4, 4) else shards_any
    return jax.shard_map(
        body,
        mesh=mesh,
        in_specs=placed,
        out_specs=P(("groups", "replica"), "tensor"),
        check_vma=False,
    )
```

time: 237 us -> 133 us (0.56)
  Pallas kernels: 0 us -> 118 us
  matrix products: 66.1 us -> 0 us
  waiting for transfers between devices: 54.8 us -> 0 us
  starting transfers between devices: 40.7 us -> 0 us
  blocking collectives: 30.1 us -> 0 us
  between operations: 14.3 us -> 0.03 us
  local copies, waits for them, and re-layouts: 25.6 us -> 14 us
  other arithmetic: 4.17 us -> 0.18 us
    pallas_call x0 -> x1, Pallas kernels: none -> 118 us  [shards_line4(): pl.pallas_call(line4_kernel, out_shape=jax.ShapeDtypeStruct((rows, cols),...]
    dot_general x29 -> x0, matrix products: 66.1 us -> none  [the longest x24 55.2 us: dot(): return jnp.dot(a, b, preferred_element_type=jnp.float32)]
    ppermute x23 -> x0, waiting for transfers between devices: 54.7 us -> none  [the longest x4 29.5 us: shards_line4(): lax.ppermute(helped.astype(jnp.bfloat16), 'tensor', [(1, 0), (2, 3)])]
    ppermute x23 -> x0, starting transfers between devices: 40.7 us -> none  [the longest x4 18.8 us: shards_line4(): from_left = lax.ppermute(mine, 'tensor', right)]
    psum x1 -> x0, blocking collectives: 30.1 us -> none  [adapter_term(): shrink_round = lax.psum(partial, 'tensor').astype(jnp.bfloat16)]
    gather x8 -> x2, local copies, waits for them, and re-layouts: 18.1 us -> 5.75 us  [the longest x1 4.16 us: shards_line4(): adapter_down[wanted].reshape(4, 2, depth, rank).transpose(0, 2, 1, 3)]
    reshape x0 -> x1, local copies, waits for them, and re-layouts: none -> 3.96 us  [shards_line4(): adapter_down[wanted].reshape(4, 2, depth, rank).transpose(0, 2, 1, 3)]
    slice x1 -> x0, local copies, waits for them, and re-layouts: 2.89 us -> none  [shards_line4(): mine = tokens[c * step:(c + 1) * step]]
  transfers between devices with their start and end apart: 24 -> 0, of which waited for: 8 -> 0; matrix products, arithmetic and copies ran while one was open for 35% -> 0% of each run, Pallas kernels for 0% -> 0%
where the time goes in v2:
time: 133 us; the launch traced here: 132 us
  Pallas kernels  118 us (89%)
  local copies, waits for them, and re-layouts  14 us (11%)
    pallas_call x1, Pallas kernels, shards_line4(): pl.pallas_call(line4_kernel, out_shape=jax.ShapeDtypeStruct((rows, cols),...  118 us
    gather x1, local copies, waits for them, and re-layouts, shards_line4(): adapter_down[wanted].reshape(4, 2, depth, rank).transpose(0, 2, 1, 3)  4.16 us
    reshape x1, local copies, waits for them, and re-layouts, shards_line4(): adapter_down[wanted].reshape(4, 2, depth, rank).transpose(0, 2, 1, 3)  3.96 us

profile of v2, /device:TPU:0, one launch (start us, length us, event | category | flops | bytes accessed | tf_op | source)
XLA Modules:
  0.0 132.2 jit_solution(17171641126953553516)
XLA Ops:
  0.0 0.0 copy-start
  0.0 1.1 dynamic-slice_reduce_fusion.3
  1.1 0.1 fusion.2
  1.2 4.2 %gather_fusion = bf16[8,2048,64]{1,2,0:T(8,128)(2,1)} fusion(bf16[16,2048,64]{1,2,0:T(8,128)(2,1)} %param.9, s32[1024]{0:T(1024)S(1)} %pad_clamp_fusion), kind=kCustom, calls=%fused_computation | custom fusion | bytes 4194336 | tf_op jit(solution)/shard_map/gather | solution.py:329
  5.4 4.0 %copy.9.down_send = bf16[4,2048,128]{2,1,0:T(8,128)(2,1)} copy(bf16[4,2048,128]{1,2,0:T(8,128)(2,1)} %bitcast.12) | data formatting | bytes 4194304 | tf_op jit(solution)/shard_map/reshape | solution.py:329
  9.3 0.0 copy-done
  9.3 0.0 copy-start.2
  9.3 0.0 copy-start.1
  9.3 1.6 %gather_fusion.1 = bf16[8,64,1024]{2,1,0:T(8,128)(2,1)} fusion(bf16[16,64,1024]{2,1,0:T(8,128)(2,1)S(1)} %copy-done, s32[1024]{0:T(1024)S(1)} %pad_clamp_fusion), kind=kCustom, calls=%fused_computation.1 | custom fusion | bytes 2097184 | tf_op jit(solution)/shard_map/gather | solution.py:330
  10.9 0.0 copy-done.2
  10.9 0.0 copy-done.1
  10.9 0.1 fusion
  11.0 0.1 select_n.58
  11.1 0.9 broadcast_in_dim.24.code
  11.9 118.0 %shard_map.73 = bf16[512,1024]{1,0:T(8,128)(2,1)} custom-call(bf16[512,2048]{1,0:T(8,128)(2,1)} %tokens.1, bf16[8192,1024]{1,0:T(8,128)(2,1)} %weight.1, bf16[4,2048,128]{2,1,0:T(8,128)(2,1)} %copy.9.down_send, bf16[4,128,1024]{2,1,0:T(8,128)(2,1)} %bitcast.13, s32[512,128]{1,0:T(8,128)} %broadcast_in_dim.24.code), custom_call_target="tpu_custom_call" | custom-call | flops 12999999488 | bytes 41943040 | tf_op jit(solution)/shard_map/pallas_call | solution.py:339
  130.0 2.3 %copy.11 = bf16[512,1024]{1,0:T(8,128)(2,1)} copy(bf16[512,1024]{1,0:T(8,128)(2,1)} %shard_map.73) | data formatting | bytes 2097152
  (2 shorter events, 0.0 us)
Async XLA Ops:
  0.0 9.3 %copy-start = (bf16[16,64,1024]{2,1,0:T(8,128)(2,1)S(1)}, bf16[16,64,1024]{2,1,0:T(8,128)(2,1)}, u32[]{:S(2)}) copy-start(bf16[16,64,1024]{2,1,0:T(8,128)(2,1)} %param.10) | copy-start | bytes 6291460
  9.3 1.6 %copy-start.2 = (s32[16]{0:T(128)S(1)}, s32[16]{0:T(128)}, u32[]{:S(2)}) copy-start(s32[16]{0:T(128)} %param.12) | copy-start | bytes 196
  9.3 1.6 %copy-start.1 = (s32[16]{0:T(128)S(1)}, s32[16]{0:T(128)}, u32[]{:S(2)}) copy-start(s32[16]{0:T(128)} %param.13) | copy-start | bytes 196

commit v3 on v2

--- a/solution.py
+++ b/solution.py
@@ -5,17 +5,17 @@
 from jax.experimental.pallas import tpu as pltpu
 from jax.sharding import PartitionSpec as P
 
-CHUNKS = 4
+CHUNKS = 8
 TILE = 256
 MESH = pl.DeviceIdType.MESH
 
 DOWN, UP, PIECE = 0, 3, 6
-ALONG_X, ALONG_Y, MATE = 7, 8, 9
-X_THEN_Y, Y_THEN_X = 10, 11
-MATE_X, MATE_Y, MATE_D0, MATE_D1 = 12, 13, 14, 15
-NEAR_END, NEAR_MID, SHRINK = 16, 17, 18
-OUTER, FORWARD, HELPED = 21, 21 + CHUNKS, 21 + 2 * CHUNKS
-COPIES = 21 + 3 * CHUNKS
+ALONG_X, ALONG_Y, MATE = 8, 10, 12
+X_THEN_Y, Y_THEN_X = 13, 14
+MATE_X, MATE_Y, MATE_D0, MATE_D1 = 15, 16, 17, 18
+NEAR_END, NEAR_MID, SHRINK = 19, 20, 21
+OUTER, FORWARD, HELPED = 24, 24 + CHUNKS, 24 + 2 * CHUNKS
+COPIES = 24 + 3 * CHUNKS
 
 
 def exchange_adapters(adapter_down, adapter_up, send_table):
@@ -73,9 +73,9 @@
 
 
 def line4_kernel(
-    tokens, weight, down_send, up_send, code, out,
+    tokens, weight, adapter_down, adapter_up, send_table, block_slot, live_rows, out,
     w, help_w, own, near, outer, distant, acc, acc_h, h_send, h_recv, downs, ups, spread, shr,
-    send, recv, local,
+    code, down_all, up_all, down_send, up_send, send, recv, local,
 ):
     g, r, t = lax.axis_index("groups"), lax.axis_index("replica"), lax.axis_index("tensor")
     rows, depth = own.shape
@@ -106,8 +106,10 @@
         return pltpu.make_async_copy(weight.at[block(i)], w.at[block(i)], local.at[n])
 
     local_own = pltpu.make_async_copy(tokens, own, local.at[4])
-    local_down = pltpu.make_async_copy(down_send.at[0], downs.at[0], local.at[5])
-    local_up = pltpu.make_async_copy(up_send.at[0], ups.at[0], local.at[6])
+    local_down = pltpu.make_async_copy(adapter_down, down_all, local.at[5])
+    local_up = pltpu.make_async_copy(adapter_up, up_all, local.at[6])
+    local_down.start()
+    local_up.start()
     local_own.start()
     loads = [load_w(n, lax.rem(t + n, 4)) for n in range(4)]
     loads[0].start()
@@ -129,11 +131,20 @@
     rx, gy, rc = r ^ 2, 1 - g, r ^ 1
     px, py, pd = g * 4 + rx, gy * 4 + r, gy * 4 + rx
     piece_row = jnp.where(g == 0, near_at, far_at) * depth + r * each
-    piece = remote(
-        PIECE, weight.at[pl.ds(pl.multiple_of(piece_row, each), each)], spot(peer), tensor=inner
-    )
-    along_x = remote(ALONG_X, spot(peer), spot(peer), replica=rx)
-    along_y = remote(ALONG_Y, spot(peer), spot(peer), groups=gy)
+    half_piece = each // 2
+    pieces = [
+        remote(
+            PIECE + h,
+            weight.at[pl.ds(pl.multiple_of(piece_row + h * half_piece, half_piece), half_piece)],
+            spot(peer, h),
+            tensor=inner,
+        )
+        for h in range(2)
+    ]
+    along_x = [remote(ALONG_X + h, spot(peer, h), spot(peer, h), replica=rx) for h in range(2)]
+    along_y = [remote(ALONG_Y + h, spot(peer, h), spot(peer, h), groups=gy) for h in range(2)]
+    from_x = [remote(ALONG_X + h, spot(px, h), spot(px, h), replica=rx) for h in range(2)]
+    from_y = [remote(ALONG_Y + h, spot(py, h), spot(py, h), groups=gy) for h in range(2)]
     mate = remote(MATE, spot(peer), spot(peer), replica=rc)
     x_then_y = remote(X_THEN_Y, spot(px, 0), spot(px, 0), groups=gy)
     y_then_x = remote(Y_THEN_X, spot(py, 1), spot(py, 1), replica=rx)
@@ -148,11 +159,11 @@
     helped = [remote(HELPED + c, h_send.at[part(c)], h_recv.at[part(c)], tensor=edge) for c in range(CHUNKS)]
     adapters = []
     for k in (2, 3, 1):
-        adapters.append(remote(DOWN + k - 1, down_send.at[k], downs.at[k], replica=r ^ k))
-        adapters.append(remote(UP + k - 1, up_send.at[k], ups.at[k], replica=r ^ k))
-    shrinks = [
-        remote(SHRINK + d - 1, shr.at[t], shr.at[t], tensor=lax.rem(t + d, 4)) for d in range(1, 4)
-    ]
+        adapters.append(remote(DOWN + k - 1, down_send.at[k - 1], downs.at[k], replica=r ^ k))
+        adapters.append(remote(UP + k - 1, up_send.at[k - 1], ups.at[k], replica=r ^ k))
+    shrink_in = remote(SHRINK, shr.at[0], shr.at[1], tensor=inner)
+    shrink_mid = remote(SHRINK + 1, shr.at[2], shr.at[3], tensor=other)
+    shrink_out = remote(SHRINK + 2, shr.at[4], shr.at[4], tensor=edge)
 
     def product(x, x_rows, weights, w_rows, put):
         def tile(n, carry):
@@ -181,27 +192,47 @@
 
     low = lax.broadcasted_iota(jnp.int32, (rows, 128), 1) < 64
 
-    def shrink_send():
+    def pick_adapters():
+        local_down.wait()
+        local_up.wait()
+        for k in range(4):
+            for c in range(2):
+                wanted = send_table[r, r ^ k, c]
+                down, up = down_all[wanted], up_all[wanted]
+                if k:
+                    down_send[k - 1, c * 64 : (c + 1) * 64] = down
+                    up_send[k - 1, c * 64 : (c + 1) * 64] = up
+                else:
+                    downs[0, c * 64 : (c + 1) * 64] = down
+                    ups[0, c * 64 : (c + 1) * 64] = up
+        for copy in adapters:
+            copy.start()
+
+    def write_codes():
+        count = block_slot.shape[0]
+        size = rows // count
+        row = lax.broadcasted_iota(jnp.int32, (size, 128), 0)
+        for b in range(count):
+            slot = block_slot[b]
+            place = ((slot >> 1) ^ r) * 2 + (slot & 1)
+            code[b * size : (b + 1) * size, :] = jnp.where(row < live_rows[b], place, -1)
+
+    def partial_shrink():
         for copy in adapters:
             copy.wait_recv()
-        local_down.wait()
         total = jnp.zeros((rows, 128), jnp.float32)
         for k in range(4):
-            value = jnp.dot(own[...], downs[k], preferred_element_type=jnp.float32)
+            value = lax.dot_general(
+                own[...], downs[k], (((1,), (1,)), ((), ())), preferred_element_type=jnp.float32
+            )
             hit = code[...] == jnp.where(low, 2 * k, 2 * k + 1)
             total = total + jnp.where(hit, value, 0.0)
         both = total + pltpu.roll(total, 64, 1)
         half = rows // 2
-        shr[t] = jnp.where(low[:half], both[:half], both[half:])
-        for copy in shrinks:
-            copy.start()
+        shr[0] = jnp.where(low[:half], both[:half], both[half:])
 
     def add_delta():
-        for d in range(1, 4):
-            from_t = lax.rem(t + 4 - d, 4)
-            remote(SHRINK + d - 1, shr.at[from_t], shr.at[from_t], tensor=lax.rem(t + d, 4)).wait_recv()
-        local_up.wait()
-        total = (shr[0] + shr[1]) + (shr[2] + shr[3])
+        total = shr[4]
         turned = pltpu.roll(total, 64, 1)
         half = rows // 2
         top = low[:half]
@@ -224,70 +255,85 @@
 
     @pl.when(is_end)
     def _():
-        piece.start()
+        pieces[0].start()
+        pieces[1].start()
 
     @pl.when(is_mid)
     def _():
         near_mid.start()
         near_end.start()
 
-    for copy in adapters:
-        copy.start()
-    local_down.start()
-    local_up.start()
+    pick_adapters()
     for load in loads[1:]:
         load.start()
+    write_codes()
     own_base()
     for load in loads[1:]:
         load.wait()
 
     @pl.when(is_end)
     def _():
-        piece.wait_send()
+        def follow(c):
+            to_inner[c - 2].wait_send()
+            to_inner[c].start()
+
+        pieces[0].wait_send()
         to_inner[0].start()
+        pieces[1].wait_send()
         to_inner[1].start()
-        to_inner[0].wait_send()
-        to_inner[2].start()
-        to_inner[1].wait_send()
-        to_inner[3].start()
-        shrink_send()
+        for c in range(2, CHUNKS - 2):
+            follow(c)
+        partial_shrink()
+        shrink_in.start()
+        for c in range(CHUNKS - 2, CHUNKS):
+            follow(c)
         near_end.wait_recv()
         add_base(near, everything, inner_at)
+        shrink_out.wait_recv()
         add_delta()
         for c in range(CHUNKS):
             helped[c].wait_recv()
             out[part(c), :] = (acc[part(c), :] + h_recv[part(c), :].astype(jnp.float32)).astype(out.dtype)
-        to_inner[2].wait_send()
-        to_inner[3].wait_send()
+        to_inner[CHUNKS - 2].wait_send()
+        to_inner[CHUNKS - 1].wait_send()
+        shrink_in.wait_send()
 
     @pl.when(is_mid)
     def _():
-        piece.wait_recv()
-        along_x.start()
-        along_y.start()
+        def relay(*chunks):
+            for c in chunks:
+                to_inner[c].wait_recv()
+                forward[c].start()
+
+        for h in range(2):
+            pieces[h].wait_recv()
+            along_x[h].start()
+            along_y[h].start()
         mate.start()
-        to_inner[0].wait_recv()
-        forward[0].start()
-        remote(ALONG_X, spot(px), spot(px), replica=rx).wait_recv()
+        from_x[0].wait_recv()
         x_then_y.start()
-        mate_x.start()
-        remote(ALONG_Y, spot(py), spot(py), groups=gy).wait_recv()
+        relay(0, 1)
+        from_y[0].wait_recv()
+        from_y[1].wait_recv()
         y_then_x.start()
         mate_y.start()
-        to_inner[1].wait_recv()
-        forward[1].start()
-        shrink_send()
+        relay(2)
+        from_x[1].wait_recv()
+        mate_x.start()
+        relay(3)
+        partial_shrink()
         near_mid.wait_recv()
         add_base(near, everything, inner_at)
-        to_inner[2].wait_recv()
-        forward[2].start()
+        relay(4)
         remote(X_THEN_Y, spot(pd, 0), spot(pd, 0), groups=gy).wait_recv()
         mate_d0.start()
         remote(Y_THEN_X, spot(pd, 1), spot(pd, 1), replica=rx).wait_recv()
         mate_d1.start()
-        to_inner[3].wait_recv()
-        forward[3].start()
-        add_base(outer, everything, edge)
+        relay(5)
+        shrink_in.wait_recv()
+        shr[2] = shr[0] + shr[1]
+        shrink_mid.start()
+        relay(6)
         pc = g * 4 + rc
         remote(MATE, spot(pc), spot(pc), replica=rc).wait_recv()
         remote(MATE_X, spot(pc ^ 2), spot(pc ^ 2), replica=rc).wait_recv()
@@ -295,13 +341,17 @@
         qd = gy * 4 + (rc ^ 2)
         remote(MATE_D0, spot(qd, 0), spot(qd, 0), replica=rc).wait_recv()
         remote(MATE_D1, spot(qd, 1), spot(qd, 1), replica=rc).wait_recv()
+        relay(7)
 
         def put_near(cols, value):
             acc_h[:, cols] = value
 
         product(near, everything, help_w, pl.ds(0, depth), put_near)
-        add_delta()
-        for c in range(CHUNKS):
+        shrink_mid.wait_recv()
+        shr[4] = shr[2] + shr[3]
+        shrink_out.start()
+
+        def help_edge(c):
             forward[c].wait_recv()
 
             def put_far(cols, value):
@@ -309,37 +359,44 @@
 
             product(distant, part(c), help_w, pl.ds(depth, depth), put_far)
             helped[c].start()
+
+        def finish(c):
             add_base(distant, part(c), 3 - edge)
             out[part(c), :] = acc[part(c), :].astype(out.dtype)
-        for copy in [near_mid, near_end, along_x, along_y, mate, x_then_y, y_then_x]:
+
+        help_edge(0)
+        help_edge(1)
+        add_base(outer, everything, edge)
+        help_edge(2)
+        add_delta()
+        help_edge(3)
+        for c in range(4):
+            finish(c)
+        for c in range(4, CHUNKS):
+            help_edge(c)
+            finish(c)
+        for copy in [near_mid, near_end, mate, x_then_y, y_then_x, shrink_mid, shrink_out]:
             copy.wait_send()
-        for copy in [mate_x, mate_y, mate_d0, mate_d1] + forward + helped:
+        for copy in along_x + along_y + [mate_x, mate_y, mate_d0, mate_d1] + forward + helped:
             copy.wait_send()
 
-    for copy in adapters + shrinks:
+    for copy in adapters:
         copy.wait_send()
 
 
 def shards_line4(tokens, query_weight, adapter_down, adapter_up, send_table, block_slot, live_block_rows):
-    me = lax.axis_index("replica")
     rows, depth = tokens.shape
     cols = query_weight.shape[1]
     rank = adapter_down.shape[2]
-    wanted = jnp.concatenate([send_table[me, me ^ k] for k in range(4)])
-    down_send = adapter_down[wanted].reshape(4, 2, depth, rank).transpose(0, 2, 1, 3).reshape(4, depth, 2 * rank)
-    up_send = adapter_up[wanted].reshape(4, 2 * rank, cols)
-    count = block_slot.shape[0]
-    place = ((block_slot // 2) ^ me) * 2 + block_slot % 2
-    live = jnp.arange(rows // count, dtype=jnp.int32)[None, :] < live_block_rows[:, None]
-    code = jnp.where(live, place[:, None], -1).reshape(rows, 1)
-    code = jnp.broadcast_to(code, (rows, 128))
+    adapter_down = adapter_down.transpose(0, 2, 1)
     bf16, f32 = jnp.bfloat16, jnp.float32
     any_space = pl.BlockSpec(memory_space=pl.ANY)
     vmem = pl.BlockSpec(memory_space=pltpu.VMEM)
+    smem = pl.BlockSpec(memory_space=pltpu.SMEM)
     return pl.pallas_call(
         line4_kernel,
         out_shape=jax.ShapeDtypeStruct((rows, cols), bf16),
-        in_specs=[any_space] * 4 + [vmem],
+        in_specs=[any_space] * 4 + [smem] * 3,
         out_specs=vmem,
         scratch_shapes=[
             pltpu.VMEM((4 * depth, cols), bf16),
@@ -352,19 +409,24 @@
             pltpu.VMEM((rows, cols), f32),
             pltpu.VMEM((rows, cols), bf16),
             pltpu.VMEM((rows, cols), bf16),
-            pltpu.VMEM((4, depth, 2 * rank), bf16),
+            pltpu.VMEM((4, 2 * rank, depth), bf16),
             pltpu.VMEM((4, 2 * rank, cols), bf16),
             pltpu.VMEM((rows, 8 * rank), bf16),
-            pltpu.VMEM((4, rows // 2, 128), f32),
+            pltpu.VMEM((5, rows // 2, 128), f32),
+            pltpu.VMEM((rows, 128), jnp.int32),
+            pltpu.VMEM(adapter_down.shape, bf16),
+            pltpu.VMEM(adapter_up.shape, bf16),
+            pltpu.VMEM((3, 2 * rank, depth), bf16),
+            pltpu.VMEM((3, 2 * rank, cols), bf16),
             pltpu.SemaphoreType.DMA((COPIES,)),
             pltpu.SemaphoreType.DMA((COPIES,)),
             pltpu.SemaphoreType.DMA((7,)),
         ],
         compiler_params=pltpu.CompilerParams(
-            collective_id=0, has_side_effects=True, vmem_limit_bytes=56 << 20
+            collective_id=0, has_side_effects=True, vmem_limit_bytes=60 << 20
         ),
         cost_estimate=pl.CostEstimate(flops=13 * 10**9, bytes_accessed=40 << 20, transcendentals=0),
-    )(tokens, query_weight, down_send, up_send, code)
+    )(tokens, query_weight, adapter_down, adapter_up, send_table, block_slot, live_block_rows)
 
 
 def solution(mesh):

time: 133 us -> 128 us (0.962)
  local copies, waits for them, and re-layouts: 14 us -> 3.64 us
  Pallas kernels: 118 us -> 124 us
    pallas_call x1, Pallas kernels: 118 us -> 124 us  [shards_line4(): pl.pallas_call(line4_kernel, out_shape=jax.ShapeDtypeStruct((rows, cols),...]
    gather x2 -> x0, local copies, waits for them, and re-layouts: 5.75 us -> none  [the longest x1 4.16 us: shards_line4(): adapter_down[wanted].reshape(4, 2, depth, rank).transpose(0, 2, 1, 3)]
    reshape x1 -> x0, local copies, waits for them, and re-layouts: 3.96 us -> none  [shards_line4(): adapter_down[wanted].reshape(4, 2, depth, rank).transpose(0, 2, 1, 3)]
    unnamed x7 -> x2, local copies, waits for them, and re-layouts: 2.27 us -> 3.64 us
where the time goes in v3:
time: 128 us; the launch traced here: 127 us
  Pallas kernels  124 us (97%)
  local copies, waits for them, and re-layouts  3.64 us (3%)
    pallas_call x1, Pallas kernels, shards_line4(): pl.pallas_call(line4_kernel, out_shape=jax.ShapeDtypeStruct((rows, cols),...  124 us
    unnamed x2, local copies, waits for them, and re-layouts  3.64 us

profile of v3, /device:TPU:0, one launch (start us, length us, event | category | flops | bytes accessed | tf_op | source)
XLA Modules:
  0.0 127.5 jit_solution(17281410750571403086)
XLA Ops:
  0.0 1.4 %copy.8.send_table = s32[4,4,2]{2,1,0:T(4,128)} copy(s32[4,4,2]{1,2,0:T(2,128)} %param.11) | data formatting | bytes 256 | tf_op args[4]
  1.4 123.8 %shard_map.73 = bf16[512,1024]{1,0:T(8,128)(2,1)} custom-call(bf16[512,2048]{1,0:T(8,128)(2,1)} %tokens.1, bf16[8192,1024]{1,0:T(8,128)(2,1)} %weight.1, bf16[16,64,2048]{2,1,0:T(8,128)(2,1)} %bitcast.1, bf16[16,64,1024]{2,1,0:T(8,128)(2,1)} %adapter_up.1, s32[4,4,2]{2,1,0:T(4,128)} %copy.8.send_table, s32[16]{0:T(128)} %block_slot.1, s32[16]{0:T(128)} %live_rows.1), custom_call_target="tpu_custom_call" | custom-call | flops 12999999488 | bytes 41943040 | tf_op jit(solution)/shard_map/pallas_call | solution.py:396
  125.2 2.3 %copy.10 = bf16[512,1024]{1,0:T(8,128)(2,1)} copy(bf16[512,1024]{1,0:T(8,128)(2,1)} %shard_map.73) | data formatting | bytes 2097152

commit v4 on v3

--- a/solution.py
+++ b/solution.py
@@ -7,6 +7,7 @@
 
 CHUNKS = 8
 TILE = 256
+GROUPS = ((0, 4), (4, 2), (6, 1), (7, 1))
 MESH = pl.DeviceIdType.MESH
 
 DOWN, UP, PIECE = 0, 3, 6
@@ -156,7 +157,11 @@
     near_mid = remote(NEAR_MID, tokens, near, tensor=other)
     to_inner = [remote(OUTER + c, tokens.at[part(c)], outer.at[part(c)], tensor=inner) for c in range(CHUNKS)]
     forward = [remote(FORWARD + c, outer.at[part(c)], distant.at[part(c)], tensor=other) for c in range(CHUNKS)]
-    helped = [remote(HELPED + c, h_send.at[part(c)], h_recv.at[part(c)], tensor=edge) for c in range(CHUNKS)]
+    group_rows = [pl.ds(c * step, n * step) for c, n in GROUPS]
+    helped = [
+        remote(HELPED + i, h_send.at[rows_of], h_recv.at[rows_of], tensor=edge)
+        for i, rows_of in enumerate(group_rows)
+    ]
     adapters = []
     for k in (2, 3, 1):
         adapters.append(remote(DOWN + k - 1, down_send.at[k - 1], downs.at[k], replica=r ^ k))
@@ -205,7 +210,12 @@
                 else:
                     downs[0, c * 64 : (c + 1) * 64] = down
                     ups[0, c * 64 : (c + 1) * 64] = up
-        for copy in adapters:
+        adapters[0].start()
+        adapters[4].start()
+        adapters[5].start()
+
+    def later_adapters():
+        for copy in adapters[1:4]:
             copy.start()
 
     def write_codes():
@@ -277,6 +287,7 @@
             to_inner[c - 2].wait_send()
             to_inner[c].start()
 
+        later_adapters()
         pieces[0].wait_send()
         to_inner[0].start()
         pieces[1].wait_send()
@@ -291,9 +302,9 @@
         add_base(near, everything, inner_at)
         shrink_out.wait_recv()
         add_delta()
-        for c in range(CHUNKS):
-            helped[c].wait_recv()
-            out[part(c), :] = (acc[part(c), :] + h_recv[part(c), :].astype(jnp.float32)).astype(out.dtype)
+        for copy, rows_of in zip(helped, group_rows):
+            copy.wait_recv()
+            out[rows_of, :] = (acc[rows_of, :] + h_recv[rows_of, :].astype(jnp.float32)).astype(out.dtype)
         to_inner[CHUNKS - 2].wait_send()
         to_inner[CHUNKS - 1].wait_send()
         shrink_in.wait_send()
@@ -310,6 +321,7 @@
             along_x[h].start()
             along_y[h].start()
         mate.start()
+        later_adapters()
         from_x[0].wait_recv()
         x_then_y.start()
         relay(0, 1)
@@ -321,19 +333,18 @@
         from_x[1].wait_recv()
         mate_x.start()
         relay(3)
-        partial_shrink()
         near_mid.wait_recv()
         add_base(near, everything, inner_at)
-        relay(4)
+        relay(4, 5)
         remote(X_THEN_Y, spot(pd, 0), spot(pd, 0), groups=gy).wait_recv()
         mate_d0.start()
         remote(Y_THEN_X, spot(pd, 1), spot(pd, 1), replica=rx).wait_recv()
         mate_d1.start()
-        relay(5)
+        relay(6, 7)
+        partial_shrink()
         shrink_in.wait_recv()
         shr[2] = shr[0] + shr[1]
         shrink_mid.start()
-        relay(6)
         pc = g * 4 + rc
         remote(MATE, spot(pc), spot(pc), replica=rc).wait_recv()
         remote(MATE_X, spot(pc ^ 2), spot(pc ^ 2), replica=rc).wait_recv()
@@ -341,40 +352,42 @@
         qd = gy * 4 + (rc ^ 2)
         remote(MATE_D0, spot(qd, 0), spot(qd, 0), replica=rc).wait_recv()
         remote(MATE_D1, spot(qd, 1), spot(qd, 1), replica=rc).wait_recv()
-        relay(7)
 
         def put_near(cols, value):
             acc_h[:, cols] = value
 
         product(near, everything, help_w, pl.ds(0, depth), put_near)
+
+        def help_edge(i):
+            c, n = GROUPS[i]
+            for at in range(c, c + n):
+                forward[at].wait_recv()
+            rows_of = group_rows[i]
+
+            def put_far(cols, value):
+                h_send[rows_of, cols] = (acc_h[rows_of, cols] + value).astype(jnp.bfloat16)
+
+            product(distant, rows_of, help_w, pl.ds(depth, depth), put_far)
+            helped[i].start()
+
+        def finish(i):
+            rows_of = group_rows[i]
+            add_base(distant, rows_of, 3 - edge)
+            out[rows_of, :] = acc[rows_of, :].astype(out.dtype)
+
+        help_edge(0)
         shrink_mid.wait_recv()
         shr[4] = shr[2] + shr[3]
         shrink_out.start()
-
-        def help_edge(c):
-            forward[c].wait_recv()
-
-            def put_far(cols, value):
-                h_send[part(c), cols] = (acc_h[part(c), cols] + value).astype(jnp.bfloat16)
-
-            product(distant, part(c), help_w, pl.ds(depth, depth), put_far)
-            helped[c].start()
-
-        def finish(c):
-            add_base(distant, part(c), 3 - edge)
-            out[part(c), :] = acc[part(c), :].astype(out.dtype)
-
-        help_edge(0)
+        add_base(outer, everything, edge)
+        add_delta()
         help_edge(1)
-        add_base(outer, everything, edge)
+        finish(0)
         help_edge(2)
-        add_delta()
+        finish(1)
         help_edge(3)
-        for c in range(4):
-            finish(c)
-        for c in range(4, CHUNKS):
-            help_edge(c)
-            finish(c)
+        finish(2)
+        finish(3)
         for copy in [near_mid, near_end, mate, x_then_y, y_then_x, shrink_mid, shrink_out]:
             copy.wait_send()
         for copy in along_x + along_y + [mate_x, mate_y, mate_d0, mate_d1] + forward + helped:

time: 128 us -> 125 us (0.977)
  Pallas kernels: 124 us -> 121 us
    pallas_call x1, Pallas kernels: 124 us -> 121 us  [shards_line4(): pl.pallas_call(line4_kernel, out_shape=jax.ShapeDtypeStruct((rows, cols),...]
where the time goes in v4:
time: 125 us; the launch traced here: 124 us
  Pallas kernels  121 us (97%)
  local copies, waits for them, and re-layouts  3.64 us (3%)
    pallas_call x1, Pallas kernels, shards_line4(): pl.pallas_call(line4_kernel, out_shape=jax.ShapeDtypeStruct((rows, cols),...  121 us
    unnamed x2, local copies, waits for them, and re-layouts  3.64 us

profile of v4, /device:TPU:0, one launch (start us, length us, event | category | flops | bytes accessed | tf_op | source)
XLA Modules:
  0.0 124.3 jit_solution(3510807314119319569)
XLA Ops:
  0.0 1.4 %copy.8.send_table = s32[4,4,2]{2,1,0:T(4,128)} copy(s32[4,4,2]{1,2,0:T(2,128)} %param.11) | data formatting | bytes 256 | tf_op args[4]
  1.4 120.7 %shard_map.73 = bf16[512,1024]{1,0:T(8,128)(2,1)} custom-call(bf16[512,2048]{1,0:T(8,128)(2,1)} %tokens.1, bf16[8192,1024]{1,0:T(8,128)(2,1)} %weight.1, bf16[16,64,2048]{2,1,0:T(8,128)(2,1)} %bitcast.1, bf16[16,64,1024]{2,1,0:T(8,128)(2,1)} %adapter_up.1, s32[4,4,2]{2,1,0:T(4,128)} %copy.8.send_table, s32[16]{0:T(128)} %block_slot.1, s32[16]{0:T(128)} %live_rows.1), custom_call_target="tpu_custom_call" | custom-call | flops 12999999488 | bytes 41943040 | tf_op jit(solution)/shard_map/pallas_call | solution.py:409
  122.0 2.3 %copy.10 = bf16[512,1024]{1,0:T(8,128)(2,1)} copy(bf16[512,1024]{1,0:T(8,128)(2,1)} %shard_map.73) | data formatting | bytes 2097152

commit v5 on v4

--- a/solution.py
+++ b/solution.py
@@ -341,10 +341,7 @@
         remote(Y_THEN_X, spot(pd, 1), spot(pd, 1), replica=rx).wait_recv()
         mate_d1.start()
         relay(6, 7)
-        partial_shrink()
-        shrink_in.wait_recv()
-        shr[2] = shr[0] + shr[1]
-        shrink_mid.start()
+        add_base(outer, everything, edge)
         pc = g * 4 + rc
         remote(MATE, spot(pc), spot(pc), replica=rc).wait_recv()
         remote(MATE_X, spot(pc ^ 2), spot(pc ^ 2), replica=rc).wait_recv()
@@ -375,14 +372,18 @@
             add_base(distant, rows_of, 3 - edge)
             out[rows_of, :] = acc[rows_of, :].astype(out.dtype)
 
+        partial_shrink()
+        shrink_in.wait_recv()
+        shr[2] = shr[0] + shr[1]
+        shrink_mid.start()
         help_edge(0)
+        add_base(distant, group_rows[0], 3 - edge)
         shrink_mid.wait_recv()
         shr[4] = shr[2] + shr[3]
         shrink_out.start()
-        add_base(outer, everything, edge)
+        help_edge(1)
         add_delta()
-        help_edge(1)
-        finish(0)
+        out[group_rows[0], :] = acc[group_rows[0], :].astype(out.dtype)
         help_edge(2)
         finish(1)
         help_edge(3)

time: 125 us -> 121 us (0.968)
  Pallas kernels: 121 us -> 117 us
    pallas_call x1, Pallas kernels: 121 us -> 117 us  [shards_line4(): pl.pallas_call(line4_kernel, out_shape=jax.ShapeDtypeStruct((rows, cols),...]
where the time goes in v5:
time: 121 us
  Pallas kernels  117 us (97%)
  local copies, waits for them, and re-layouts  3.64 us (3%)
    pallas_call x1, Pallas kernels, shards_line4(): pl.pallas_call(line4_kernel, out_shape=jax.ShapeDtypeStruct((rows, cols),...  117 us
    unnamed x2, local copies, waits for them, and re-layouts  3.64 us

profile of v5, /device:TPU:0, one launch (start us, length us, event | category | flops | bytes accessed | tf_op | source)
XLA Modules:
  0.0 120.9 jit_solution(883503959167153854)
XLA Ops:
  0.0 1.4 %copy.8.send_table = s32[4,4,2]{2,1,0:T(4,128)} copy(s32[4,4,2]{1,2,0:T(2,128)} %param.11) | data formatting | bytes 256 | tf_op args[4]
  1.4 117.2 %shard_map.73 = bf16[512,1024]{1,0:T(8,128)(2,1)} custom-call(bf16[512,2048]{1,0:T(8,128)(2,1)} %tokens.1, bf16[8192,1024]{1,0:T(8,128)(2,1)} %weight.1, bf16[16,64,2048]{2,1,0:T(8,128)(2,1)} %bitcast.1, bf16[16,64,1024]{2,1,0:T(8,128)(2,1)} %adapter_up.1, s32[4,4,2]{2,1,0:T(4,128)} %copy.8.send_table, s32[16]{0:T(128)} %block_slot.1, s32[16]{0:T(128)} %live_rows.1), custom_call_target="tpu_custom_call" | custom-call | flops 12999999488 | bytes 41943040 | tf_op jit(solution)/shard_map/pallas_call | solution.py:410
  118.6 2.3 %copy.10 = bf16[512,1024]{1,0:T(8,128)(2,1)} copy(bf16[512,1024]{1,0:T(8,128)(2,1)} %shard_map.73) | data formatting | bytes 2097152
